TPU v7x, 32 devices: a whole 2x2x4 slice. The times are simulated.
32 devices in a mesh: dp: 8 (over z, y), sp: 4 (over x, core).
Axes of the slice: x: 2, y: 2, z: 4, core: 2. Of those that a mesh axis runs over, the one named last changes fastest.
Arguments:
- hidden_in: bfloat16 [16, 1024, 1024], P('dp', 'sp'), may hold values from -6 to 6
- time_embed: bfloat16 [16, 1024], P('dp'), may hold values from -6 to 6
- seg_lengths: int32 [16, 4], P('dp'), may hold values from 1 to 1021, as said below
- ada_weight: bfloat16 [1024, 6144], P('dp', 'sp'), may hold values from -0.1875 to 0.1875
- query_weight: bfloat16 [1024, 1024], P('dp', 'sp'), may hold values from -0.1875 to 0.1875
- key_weight: bfloat16 [1024, 1024], P('dp', 'sp'), may hold values from -0.1875 to 0.1875
- value_weight: bfloat16 [1024, 1024], P('dp', 'sp'), may hold values from -0.1875 to 0.1875
- out_weight: bfloat16 [1024, 1024], P('dp', 'sp'), may hold values from -2 to 2
- up_weight: bfloat16 [1024, 2048], P('dp', 'sp'), may hold values from -0.1875 to 0.1875
- down_weight: bfloat16 [2048, 1024], P('dp', 'sp'), may hold values from -0.125 to 0.125
- out_cotangent: bfloat16 [16, 1024, 1024], P('dp', 'sp'), may hold values from -6 to 6
Outputs:
- hidden_out: bfloat16 [16, 1024, 1024], P('dp', 'sp')
- hidden_grad: bfloat16 [16, 1024, 1024], P('dp', 'sp')
- time_grad: float32 [16, 1024], P('dp')
- ada_grad: float32 [1024, 6144], P('dp', 'sp')
- query_grad: float32 [1024, 1024], P('dp', 'sp')
- key_grad: float32 [1024, 1024], P('dp', 'sp')
- value_grad: float32 [1024, 1024], P('dp', 'sp')
- out_weight_grad: float32 [1024, 1024], P('dp', 'sp')
- up_grad: float32 [1024, 2048], P('dp', 'sp')
- down_grad: float32 [2048, 1024], P('dp', 'sp')
Inputs may be any that keep to these rules, and one draw needn't show every extreme that they name: `seg_lengths`: in every row the 4 lengths sum to 1024, and one segment, at a place drawn for each row, is longer than 768 frames.
All inputs are finite; a program needn't handle non-finite values.
Results may differ from a plain program's by a relative error of at most 0.019.
Values may be sent and summed in bfloat16 or wider, within the bound.
No kernel may reach another device: no remote copies, remote signals or barrier semaphores. Data moves between devices by JAX's collectives and lax.ppermute only.
A program may use at most 192 MiB of HBM per device.

v0:
```python
import jax
import jax.numpy as jnp
from jax import lax
from jax.sharding import PartitionSpec as P

HEAD_DIM = 64


HIGH = lax.Precision.HIGHEST


def for_sending(shard):

    def short(part):
        return part.astype(jnp.bfloat16) if part.dtype == jnp.float32 else part

    return jax.tree.map(short, shard)


def segment_info(frame_ids, lengths):
    seg_ends = jnp.cumsum(lengths)
    passed = frame_ids[:, None] >= seg_ends[None, :]
    seg_ids = jnp.sum(passed.astype(jnp.int32), axis=1)
    positions = frame_ids - jnp.sum(jnp.where(passed, lengths[None, :], 0), axis=1)
    return (seg_ids, positions)


def rotary(positions):
    half_dim = HEAD_DIM // 2
    inverse = 10000.0 ** (-jnp.arange(half_dim, dtype=jnp.float32) / half_dim)
    angles = positions.astype(jnp.float32)[:, None] * inverse[None, :]
    return (jnp.cos(angles), jnp.sin(angles))


def rotate(values, cosine, sine, head_count, turn_sign):
    frames = values.shape[0]
    split = values.reshape(frames, head_count, HEAD_DIM)
    half_dim = HEAD_DIM // 2
    first_half = split[..., :half_dim]
    second_half = split[..., half_dim:]
    cos_part = cosine[:, None, :]
    sin_part = sine[:, None, :] * turn_sign
    turned = jnp.concatenate(
        [
            first_half * cos_part - second_half * sin_part,
            second_half * cos_part + first_half * sin_part,
        ],
        axis=-1,
    )
    return turned.reshape(frames, head_count * HEAD_DIM)


def layer_norm(values):
    centre = values - jnp.mean(values, axis=-1, keepdims=True)
    spread = jnp.mean(centre * centre, axis=-1, keepdims=True)
    return centre * lax.rsqrt(spread + 1e-06)


def modulate(values, scale_vec, shift_vec):
    return layer_norm(values) * (1.0 + scale_vec) + shift_vec


def gelu_tanh(values):
    return jax.nn.gelu(values, approximate=True)


def score_block(query_block, key_split, seg_block, seg_ids, head_count):
    block_rows = query_block.shape[0]
    query_split = query_block.reshape(block_rows, head_count, HEAD_DIM)
    scores = jnp.einsum(
        "qhd,khd->hqk", query_split, key_split, preferred_element_type=jnp.float32
    ) * HEAD_DIM ** (-0.5)
    same_segment = seg_block[:, None] == seg_ids[None, :]
    return (jnp.where(same_segment[None], scores, -1e30), query_split)


def forward_row(hidden_row, time_row, lengths, weights_full):
    ada_full, query_full, key_full, value_full, out_full, up_full, down_full = weights_full
    sp_count = lax.axis_size("sp")
    sp_rank = lax.axis_index("sp")
    local_frames = hidden_row.shape[0]
    width = hidden_row.shape[1]
    frames = local_frames * sp_count
    total_heads = width // HEAD_DIM
    head_count = total_heads // sp_count
    seg_ids, _ = segment_info(jnp.arange(frames, dtype=jnp.int32), lengths)
    local_ids = sp_rank * local_frames + jnp.arange(local_frames, dtype=jnp.int32)
    _, positions = segment_info(local_ids, lengths)
    cosine, sine = rotary(positions)
    hidden = hidden_row.astype(jnp.float32)
    time_vec = time_row.astype(jnp.float32)
    time_low = jax.nn.silu(time_vec).astype(jnp.bfloat16)
    modulation = jnp.dot(time_low, ada_full, preferred_element_type=jnp.float32)
    attn_shift, attn_scale, attn_gate, ffn_shift, ffn_scale, ffn_gate = jnp.split(modulation, 6)
    attn_input = modulate(hidden, attn_scale, attn_shift).astype(jnp.bfloat16)
    query_raw = jnp.dot(attn_input, query_full, preferred_element_type=jnp.float32)
    key_raw = jnp.dot(attn_input, key_full, preferred_element_type=jnp.float32)
    value_raw = jnp.dot(attn_input, value_full, preferred_element_type=jnp.float32)
    query_rot = rotate(query_raw, cosine, sine, total_heads, 1.0).astype(jnp.bfloat16)
    key_rot = rotate(key_raw, cosine, sine, total_heads, 1.0).astype(jnp.bfloat16)
    value_low = value_raw.astype(jnp.bfloat16)
    query_heads, key_heads, value_heads = (
        lax.all_to_all(query_rot, "sp", split_axis=1, concat_axis=0, tiled=True),
        lax.all_to_all(key_rot, "sp", split_axis=1, concat_axis=0, tiled=True),
        lax.all_to_all(value_low, "sp", split_axis=1, concat_axis=0, tiled=True),
    )
    block_rows = min(512, frames)
    block_count = frames // block_rows
    key_split = key_heads.reshape(frames, head_count, HEAD_DIM)
    value_split = value_heads.reshape(frames, head_count, HEAD_DIM)
    query_blocks = query_heads.reshape(block_count, block_rows, head_count * HEAD_DIM)
    seg_blocks = seg_ids.reshape(block_count, block_rows)

    def attend(block_pair):
        query_block, seg_block = block_pair
        scores, _ = score_block(query_block, key_split, seg_block, seg_ids, head_count)
        row_max = jnp.max(scores, axis=-1, keepdims=True)
        exponent = jnp.exp(scores - row_max)
        row_total = jnp.sum(exponent, axis=-1, keepdims=True)
        soft_low = (exponent / row_total).astype(jnp.bfloat16)
        attended_block = jnp.einsum(
            "hqk,khd->qhd", soft_low, value_split, preferred_element_type=jnp.float32
        )
        log_total = (row_max + jnp.log(row_total))[..., 0]
        return (
            attended_block.reshape(block_rows, head_count * HEAD_DIM).astype(jnp.bfloat16),
            log_total,
        )

    attended_blocks, log_totals = lax.map(attend, (query_blocks, seg_blocks))
    attended_heads = attended_blocks.reshape(frames, head_count * HEAD_DIM)
    attended = lax.all_to_all(attended_heads, "sp", split_axis=0, concat_axis=1, tiled=True)
    branch_attn = jnp.dot(attended, out_full, preferred_element_type=jnp.float32)
    mid = hidden + attn_gate * branch_attn
    ffn_input = modulate(mid, ffn_scale, ffn_shift).astype(jnp.bfloat16)
    up_proj = jnp.dot(ffn_input, up_full, preferred_element_type=jnp.float32)
    gelu_low = gelu_tanh(up_proj).astype(jnp.bfloat16)
    branch_ffn = jnp.dot(gelu_low, down_full, preferred_element_type=jnp.float32)
    hidden_out = (mid + ffn_gate * branch_ffn).astype(jnp.bfloat16)
    kept = {
        "hidden": hidden,
        "time_vec": time_vec,
        "time_low": time_low,
        "attn_scale": attn_scale,
        "attn_shift": attn_shift,
        "attn_gate": attn_gate,
        "ffn_scale": ffn_scale,
        "ffn_shift": ffn_shift,
        "ffn_gate": ffn_gate,
        "attn_input": attn_input,
        "key_split": key_split,
        "value_split": value_split,
        "query_blocks": query_blocks,
        "seg_ids": seg_ids,
        "seg_blocks": seg_blocks,
        "log_totals": log_totals,
        "attended": attended,
        "branch_attn": branch_attn,
        "mid": mid,
        "ffn_input": ffn_input,
        "up_proj": up_proj,
        "gelu_low": gelu_low,
        "branch_ffn": branch_ffn,
        "cosine": cosine,
        "sine": sine,
    }
    return (hidden_out, kept)


def backward_row(kept, cotan_row, weights_full):
    ada_back, query_back, key_back, value_back, out_back, up_back, down_back = weights_full
    sp_count = lax.axis_size("sp")
    local_frames = cotan_row.shape[0]
    width = cotan_row.shape[1]
    frames = local_frames * sp_count
    total_heads = width // HEAD_DIM
    head_count = total_heads // sp_count
    block_rows = min(512, frames)
    block_count = frames // block_rows
    key_split = kept["key_split"]
    value_split = kept["value_split"]
    seg_ids = kept["seg_ids"]
    cotan = cotan_row.astype(jnp.float32)
    ffn_gate_grad = jnp.sum(cotan * kept["branch_ffn"], axis=0)
    d_branch_ffn = (cotan * kept["ffn_gate"]).astype(jnp.bfloat16)
    down_term = jnp.einsum(
        "fi,fj->ij", kept["gelu_low"], d_branch_ffn, preferred_element_type=jnp.float32
    )
    d_gelu = jnp.einsum("fj,ij->fi", d_branch_ffn, down_back, preferred_element_type=jnp.float32)
    _, gelu_pullback = jax.vjp(gelu_tanh, kept["up_proj"])
    d_up = gelu_pullback(d_gelu)[0].astype(jnp.bfloat16)
    up_term = jnp.einsum("fi,fj->ij", kept["ffn_input"], d_up, preferred_element_type=jnp.float32)
    d_ffn_input = jnp.einsum("fj,ij->fi", d_up, up_back, preferred_element_type=jnp.float32)
    _, ffn_pullback = jax.vjp(modulate, kept["mid"], kept["ffn_scale"], kept["ffn_shift"])
    d_mid_norm, ffn_scale_grad, ffn_shift_grad = ffn_pullback(d_ffn_input)
    d_mid = cotan + d_mid_norm
    attn_gate_grad = jnp.sum(d_mid * kept["branch_attn"], axis=0)
    d_branch_attn = (d_mid * kept["attn_gate"]).astype(jnp.bfloat16)
    out_term = jnp.einsum(
        "fi,fj->ij", kept["attended"], d_branch_attn, preferred_element_type=jnp.float32
    )
    d_attended = jnp.einsum(
        "fj,ij->fi", d_branch_attn, out_back, preferred_element_type=jnp.float32
    ).astype(jnp.bfloat16)
    d_attended_heads = lax.all_to_all(d_attended, "sp", split_axis=1, concat_axis=0, tiled=True)
    grad_blocks = d_attended_heads.reshape(block_count, block_rows, head_count * HEAD_DIM)
    score_scale = HEAD_DIM ** (-0.5)

    def attend_back(carry, block_args):
        d_keys, d_values = carry
        query_block, seg_block, log_block, grad_block = block_args
        scores, query_split = score_block(query_block, key_split, seg_block, seg_ids, head_count)
        soft_values = jnp.exp(scores - log_block[:, :, None])
        grad_split = grad_block.reshape(block_rows, head_count, HEAD_DIM)
        d_soft = jnp.einsum(
            "qhd,khd->hqk", grad_split, value_split, preferred_element_type=jnp.float32
        )
        row_inner = jnp.sum(d_soft * soft_values, axis=-1, keepdims=True)
        d_scores = (soft_values * (d_soft - row_inner)).astype(jnp.bfloat16)
        d_query_block = (
            jnp.einsum("hqk,khd->qhd", d_scores, key_split, preferred_element_type=jnp.float32)
            * score_scale
        )
        d_keys = (
            d_keys
            + jnp.einsum("hqk,qhd->khd", d_scores, query_split, preferred_element_type=jnp.float32)
            * score_scale
        )
        d_values = d_values + jnp.einsum(
            "hqk,qhd->khd",
            soft_values.astype(jnp.bfloat16),
            grad_split,
            preferred_element_type=jnp.float32,
        )
        return (
            (d_keys, d_values),
            d_query_block.reshape(block_rows, head_count * HEAD_DIM).astype(jnp.bfloat16),
        )

    zero_heads = jnp.zeros((frames, head_count, HEAD_DIM), jnp.float32)
    (d_keys, d_values), d_query_blocks = lax.scan(
        attend_back,
        (zero_heads, zero_heads),
        (kept["query_blocks"], kept["seg_blocks"], kept["log_totals"], grad_blocks),
    )
    d_query_heads = d_query_blocks.reshape(frames, head_count * HEAD_DIM)
    d_key_heads = d_keys.reshape(frames, head_count * HEAD_DIM).astype(jnp.bfloat16)
    d_value_heads = d_values.reshape(frames, head_count * HEAD_DIM).astype(jnp.bfloat16)
    d_query_rot, d_key_rot, d_value = (
        lax.all_to_all(d_query_heads, "sp", split_axis=0, concat_axis=1, tiled=True),
        lax.all_to_all(d_key_heads, "sp", split_axis=0, concat_axis=1, tiled=True),
        lax.all_to_all(d_value_heads, "sp", split_axis=0, concat_axis=1, tiled=True),
    )
    d_query = rotate(
        d_query_rot.astype(jnp.float32), kept["cosine"], kept["sine"], total_heads, -1.0
    ).astype(jnp.bfloat16)
    d_key = rotate(
        d_key_rot.astype(jnp.float32), kept["cosine"], kept["sine"], total_heads, -1.0
    ).astype(jnp.bfloat16)
    attn_input = kept["attn_input"]
    query_term = jnp.einsum("fi,fj->ij", attn_input, d_query, preferred_element_type=jnp.float32)
    key_term = jnp.einsum("fi,fj->ij", attn_input, d_key, preferred_element_type=jnp.float32)
    value_term = jnp.einsum("fi,fj->ij", attn_input, d_value, preferred_element_type=jnp.float32)
    d_attn_input = jnp.einsum("fj,ij->fi", d_query, query_back, preferred_element_type=jnp.float32)
    d_attn_input = d_attn_input + jnp.einsum(
        "fj,ij->fi", d_key, key_back, preferred_element_type=jnp.float32
    )
    d_attn_input = d_attn_input + jnp.einsum(
        "fj,ij->fi", d_value, value_back, preferred_element_type=jnp.float32
    )
    _, attn_pullback = jax.vjp(modulate, kept["hidden"], kept["attn_scale"], kept["attn_shift"])
    d_hidden_norm, attn_scale_grad, attn_shift_grad = attn_pullback(d_attn_input)
    hidden_grad = (d_mid + d_hidden_norm).astype(jnp.bfloat16)
    d_modulation = jnp.concatenate(
        [
            attn_shift_grad,
            attn_scale_grad,
            attn_gate_grad,
            ffn_shift_grad,
            ffn_scale_grad,
            ffn_gate_grad,
        ]
    )
    terms = (query_term, key_term, value_term, out_term, up_term, down_term)
    return (hidden_grad, d_modulation, terms)


def time_gradient(ada_back, d_modulation, time_vecs):
    d_time_low = jnp.dot(d_modulation, ada_back.astype(jnp.float32).T, precision=HIGH)
    _, silu_pullback = jax.vjp(jax.nn.silu, time_vecs)
    return silu_pullback(d_time_low)[0]


def local(
    hidden_in,
    time_embed,
    seg_lengths,
    ada_weight,
    query_weight,
    key_weight,
    value_weight,
    out_weight,
    up_weight,
    down_weight,
    out_cotangent,
):
    shards = (
        ada_weight,
        query_weight,
        key_weight,
        value_weight,
        out_weight,
        up_weight,
        down_weight,
    )
    columns = (
        lax.all_gather(shards[0], "sp", axis=1, tiled=True),
        lax.all_gather(shards[1], "sp", axis=1, tiled=True),
        lax.all_gather(shards[2], "sp", axis=1, tiled=True),
        lax.all_gather(shards[3], "sp", axis=1, tiled=True),
        lax.all_gather(shards[4], "sp", axis=1, tiled=True),
        lax.all_gather(shards[5], "sp", axis=1, tiled=True),
        lax.all_gather(shards[6], "sp", axis=1, tiled=True),
    )
    gathered = (
        lax.all_gather(columns[0], "dp", axis=0, tiled=True),
        lax.all_gather(columns[1], "dp", axis=0, tiled=True),
        lax.all_gather(columns[2], "dp", axis=0, tiled=True),
        lax.all_gather(columns[3], "dp", axis=0, tiled=True),
        lax.all_gather(columns[4], "dp", axis=0, tiled=True),
        lax.all_gather(columns[5], "dp", axis=0, tiled=True),
        lax.all_gather(columns[6], "dp", axis=0, tiled=True),
    )
    row_count = hidden_in.shape[0]
    outputs = []
    kept_rows = []
    for row in range(row_count):
        hidden_out_row, kept = forward_row(
            hidden_in[row], time_embed[row], seg_lengths[row], gathered
        )
        outputs.append(hidden_out_row)
        kept_rows.append(kept)
    columns_again = (
        lax.all_gather(shards[0], "sp", axis=1, tiled=True),
        lax.all_gather(shards[1], "sp", axis=1, tiled=True),
        lax.all_gather(shards[2], "sp", axis=1, tiled=True),
        lax.all_gather(shards[3], "sp", axis=1, tiled=True),
        lax.all_gather(shards[4], "sp", axis=1, tiled=True),
        lax.all_gather(shards[5], "sp", axis=1, tiled=True),
        lax.all_gather(shards[6], "sp", axis=1, tiled=True),
    )
    again = (
        lax.all_gather(columns_again[0], "dp", axis=0, tiled=True),
        lax.all_gather(columns_again[1], "dp", axis=0, tiled=True),
        lax.all_gather(columns_again[2], "dp", axis=0, tiled=True),
        lax.all_gather(columns_again[3], "dp", axis=0, tiled=True),
        lax.all_gather(columns_again[4], "dp", axis=0, tiled=True),
        lax.all_gather(columns_again[5], "dp", axis=0, tiled=True),
        lax.all_gather(columns_again[6], "dp", axis=0, tiled=True),
    )
    grads_rows = []
    modulation_rows = []
    term_total = None
    for row in range(row_count):
        hidden_grad_row, d_modulation, terms = backward_row(
            kept_rows[row], out_cotangent[row], again
        )
        grads_rows.append(hidden_grad_row)
        modulation_rows.append(d_modulation)
        if term_total is None:
            term_total = terms
        else:
            term_total = tuple((total + term for total, term in zip(term_total, terms)))
    d_modulations = jnp.stack(modulation_rows)
    time_lows = jnp.stack([kept["time_low"] for kept in kept_rows])
    time_vecs = jnp.stack([kept["time_vec"] for kept in kept_rows])
    hidden_out = jnp.stack(outputs)
    hidden_grad = jnp.stack(grads_rows)
    ada_term = jnp.dot(time_lows.astype(jnp.float32).T, d_modulations, precision=HIGH)
    d_time = time_gradient(again[0], d_modulations, time_vecs)
    time_grad = lax.psum(d_time, "sp")
    col_sums = jax.tree.map(
        lambda part: part.astype(jnp.float32),
        lax.psum_scatter(
            for_sending((ada_term,) + term_total), "sp", scatter_dimension=1, tiled=True
        ),
    )
    grads = jax.tree.map(
        lambda part: part.astype(jnp.float32),
        lax.psum_scatter(for_sending(col_sums), "dp", scatter_dimension=0, tiled=True),
    )
    return (
        hidden_out,
        hidden_grad,
        time_grad,
        grads[0],
        grads[1],
        grads[2],
        grads[3],
        grads[4],
        grads[5],
        grads[6],
    )


def solution(mesh):
    in_specs = (
        P("dp", "sp", None),
        P("dp", None),
        P("dp", None),
        P("dp", "sp"),
        P("dp", "sp"),
        P("dp", "sp"),
        P("dp", "sp"),
        P("dp", "sp"),
        P("dp", "sp"),
        P("dp", "sp"),
        P("dp", "sp", None),
    )
    out_specs = (
        P("dp", "sp", None),
        P("dp", "sp", None),
        P("dp", None),
        P("dp", "sp"),
        P("dp", "sp"),
        P("dp", "sp"),
        P("dp", "sp"),
        P("dp", "sp"),
        P("dp", "sp"),
        P("dp", "sp"),
    )
    return jax.shard_map(local, mesh=mesh, in_specs=in_specs, out_specs=out_specs, check_vma=False)
```

profile of v0, /device:TPU:0, one launch (start us, length us, event | category | flops | bytes accessed | tf_op | source)
XLA Modules:
  0.0 1660.8 jit_solution(13662331897630192176)
XLA Ops:
  57.3 27.6 %all-gather.15.cloned.1.call-done = bf16[1024,1024]{1,0:T(8,128)(2,1)} async-done(((bf16[128,1024]{1,0:T(8,128)(2,1)}), bf16[1024,1024]{1,0:T(8,128)(2,1)}) %all-gather.15.cloned.1.call-update) | async-done | bytes 2097168 | tf_op jit(solution)/shard_map/all_gather | solution.py:328
  87.7 47.1 %all-gather.13.cloned.1.call-done = bf16[1024,1024]{1,0:T(8,128)(2,1)} async-done(((bf16[128,1024]{1,0:T(8,128)(2,1)}), bf16[1024,1024]{1,0:T(8,128)(2,1)}) %all-gather.13.cloned.1.call-update) | async-done | bytes 2097168 | tf_op jit(solution)/shard_map/all_gather | solution.py:327
  138.7 173.1 %all-gather.11.cloned.1.call-done = bf16[1024,6144]{1,0:T(8,128)(2,1)} async-done(((bf16[128,6144]{1,0:T(8,128)(2,1)}), bf16[1024,6144]{1,0:T(8,128)(2,1)}) %all-gather.11.cloned.1.call-update) | async-done | bytes 12582928 | tf_op jit(solution)/shard_map/all_gather | solution.py:326
  337.8 23.5 %all-gather.17.cloned.1.call-done = bf16[1024,1024]{1,0:T(8,128)(2,1)} async-done(((bf16[128,1024]{1,0:T(8,128)(2,1)}), bf16[1024,1024]{1,0:T(8,128)(2,1)}) %all-gather.17.cloned.1.call-update) | async-done | bytes 2097168 | tf_op jit(solution)/shard_map/all_gather | solution.py:329
  368.1 12.9 all_gather.68
  385.2 19.8 %while.54 = (s32[]{:T(128)}, bf16[2,512,256]{2,1,0:T(8,128)(2,1)}, f32[2,4,512]{2,1,0:T(4,128)S(1)}, s32[2,512]{1,0:T(2,128)S(1)}, s32[1024]{0:T(1024)S(1)}, /*i...) while((s32[]{:T(128)}, bf16[2,512,256]{2,1,0:T(8,128)(2,1)}, ...), condition=%wide.region_8.9_spmd, body=%wide.region_5.8_spmd.sunk | while | flops 562690048 | bytes 30484596 | solution.py:130
  424.5 60.7 %all-gather.21.cloned.1.call-done = bf16[1024,2048]{1,0:T(8,128)(2,1)} async-done(((bf16[128,2048]{1,0:T(8,128)(2,1)}), bf16[1024,2048]{1,0:T(8,128)(2,1)}) %all-gather.21.cloned.1.call-update) | async-done | bytes 4194320 | tf_op jit(solution)/shard_map/all_gather | solution.py:331
  490.4 68.6 %all-gather.23.cloned.1.call-done = bf16[2048,1024]{1,0:T(8,128)(2,1)} async-done(((bf16[256,1024]{1,0:T(8,128)(2,1)}), bf16[2048,1024]{1,0:T(8,128)(2,1)}) %all-gather.23.cloned.1.call-update) | async-done | bytes 4194320 | tf_op jit(solution)/shard_map/all_gather | solution.py:332
  587.9 61.2 %while.56 = (s32[]{:T(128)}, f32[1024,4,64]{0,2,1:T(8,128)S(1)}, f32[1024,4,64]{0,2,1:T(8,128)}, bf16[2,512,256]{2,1,0:T(8,128)(2,1)}, bf16[2,512,256]{1,2,0:T(8...) while((s32[]{:T(128)}, f32[1024,4,64]{0,2,1:T(8,128)S(1)}, ...), condition=%wide.region_26.27_spmd.clone, body=%wide.region_24.26_spmd.clone.sunk | while | flops 1375729664 | bytes 126159184 | solution.py:241
  734.7 19.8 %while.55 = (s32[]{:T(128)}, bf16[2,512,256]{2,1,0:T(8,128)(2,1)}, f32[2,4,512]{2,1,0:T(4,128)S(1)}, s32[2,512]{1,0:T(2,128)S(1)}, s32[1024]{0:T(1024)S(1)}, /*i...) while((s32[]{:T(128)}, bf16[2,512,256]{2,1,0:T(8,128)(2,1)}, ...), condition=%wide.region_19.20_spmd, body=%wide.region_16.19_spmd.sunk | while | flops 562690048 | bytes 30484596 | solution.py:130
  799.8 61.5 %while.57 = (s32[]{:T(128)}, f32[1024,4,64]{0,2,1:T(8,128)S(1)}, f32[1024,4,64]{0,2,1:T(8,128)}, bf16[2,512,256]{2,1,0:T(8,128)(2,1)}, bf16[2,512,256]{1,2,0:T(8...) while((s32[]{:T(128)}, f32[1024,4,64]{0,2,1:T(8,128)S(1)}, ...), condition=%wide.region_33.34_spmd.clone, body=%wide.region_31.33_spmd.clone.sunk | while | flops 1375729664 | bytes 126159184 | solution.py:241
  941.5 12.5 convolution_convert_fusion
  955.8 32.8 %reduce-scatter.27.cloned.1.call-done = bf16[1024,256]{1,0:T(8,128)(2,1)} async-done(((bf16[1024,1024]{1,0:T(8,128)(2,1)}), bf16[1024,256]{1,0:T(8,128)(2,1)}) %reduce-scatter.27.cloned.1.call-update) | async-done | bytes 524304 | tf_op jit(solution)/shard_map/reduce_scatter | solution.py:384
  988.7 47.0 %reduce-scatter.35.cloned.1.call-done = bf16[1024,512]{1,0:T(8,128)(2,1)} async-done(((bf16[1024,2048]{1,0:T(8,128)(2,1)}), bf16[1024,512]{1,0:T(8,128)(2,1)}) %reduce-scatter.35.cloned.1.call-update) | async-done | bytes 1048592 | tf_op jit(solution)/shard_map/reduce_scatter | solution.py:384
  1035.7 47.0 %reduce-scatter.39.cloned.1.call-done = bf16[2048,256]{1,0:T(8,128)(2,1)} async-done(((bf16[2048,1024]{1,0:T(8,128)(2,1)}), bf16[2048,256]{1,0:T(8,128)(2,1)}) %reduce-scatter.39.cloned.1.call-update) | async-done | bytes 1048592 | tf_op jit(solution)/shard_map/reduce_scatter | solution.py:384
  1083.1 101.2 %reduce-scatter.15.cloned.1.call-done = bf16[1024,1536]{1,0:T(8,128)(2,1)} async-done(((bf16[1024,6144]{1,0:T(8,128)(2,1)}), bf16[1024,1536]{1,0:T(8,128)(2,1)}) %reduce-scatter.15.cloned.1.call-update) | async-done | bytes 3145744 | tf_op jit(solution)/shard_map/reduce_scatter | solution.py:384
  1186.6 12.8 fusion.145
  1210.0 39.5 %reduce-scatter.33.cloned.1.call-done = bf16[128,256]{1,0:T(8,128)(2,1)} async-done(((bf16[1024,256]{1,0:T(8,128)(2,1)}), bf16[128,256]{1,0:T(8,128)(2,1)}) %reduce-scatter.33.cloned.1.call-update) | async-done | bytes 65552 | tf_op jit(solution)/shard_map/reduce_scatter | solution.py:390
  1251.0 63.0 %reduce-scatter.21.cloned.1.call-done = bf16[128,256]{1,0:T(8,128)(2,1)} async-done(((bf16[1024,256]{1,0:T(8,128)(2,1)}), bf16[128,256]{1,0:T(8,128)(2,1)}) %reduce-scatter.21.cloned.1.call-update) | async-done | bytes 65552 | tf_op jit(solution)/shard_map/reduce_scatter | solution.py:390
  1315.5 62.7 %reduce-scatter.25.cloned.1.call-done = bf16[128,256]{1,0:T(8,128)(2,1)} async-done(((bf16[1024,256]{1,0:T(8,128)(2,1)}), bf16[128,256]{1,0:T(8,128)(2,1)}) %reduce-scatter.25.cloned.1.call-update) | async-done | bytes 65552 | tf_op jit(solution)/shard_map/reduce_scatter | solution.py:390
  1379.7 63.1 %reduce-scatter.29.cloned.1.call-done = bf16[128,256]{1,0:T(8,128)(2,1)} async-done(((bf16[1024,256]{1,0:T(8,128)(2,1)}), bf16[128,256]{1,0:T(8,128)(2,1)}) %reduce-scatter.29.cloned.1.call-update) | async-done | bytes 65552 | tf_op jit(solution)/shard_map/reduce_scatter | solution.py:390
  1444.3 64.2 %reduce-scatter.37.cloned.1.call-done = bf16[128,512]{1,0:T(8,128)(2,1)} async-done(((bf16[1024,512]{1,0:T(8,128)(2,1)}), bf16[128,512]{1,0:T(8,128)(2,1)}) %reduce-scatter.37.cloned.1.call-update) | async-done | bytes 131088 | tf_op jit(solution)/shard_map/reduce_scatter | solution.py:390
  1510.1 64.6 %reduce-scatter.41.cloned.1.call-done = bf16[256,256]{1,0:T(8,128)(2,1)} async-done(((bf16[2048,256]{1,0:T(8,128)(2,1)}), bf16[256,256]{1,0:T(8,128)(2,1)}) %reduce-scatter.41.cloned.1.call-update) | async-done | bytes 131088 | tf_op jit(solution)/shard_map/reduce_scatter | solution.py:390
  1576.4 75.4 %reduce-scatter.17.cloned.1.call-done = bf16[128,1536]{1,0:T(8,128)(2,1)} async-done(((bf16[1024,1536]{1,0:T(8,128)(2,1)}), bf16[128,1536]{1,0:T(8,128)(2,1)}) %reduce-scatter.17.cloned.1.call-update) | async-done | bytes 393232 | tf_op jit(solution)/shard_map/reduce_scatter | solution.py:390
  (633 shorter events, 544.3 us)
Async XLA Ops:
  7.2 25.1 %all-gather.9.cloned.1.call-start = ((), (), s32[]{:S(2)}) async-start(), calls=%async_computation.30 | async-start | bytes 1966080 | tf_op jit(solution)/shard_map/all_gather | solution.py:317
  8.0 76.9 %all-gather.15.cloned.1.call-start = ((), (), s32[]{:S(2)}) async-start(), calls=%async_computation.33 | async-start | bytes 2359296 | tf_op jit(solution)/shard_map/all_gather | solution.py:328
  16.9 117.9 %all-gather.13.cloned.1.call-start = ((), (), s32[]{:S(2)}) async-start(), calls=%async_computation.32 | async-start | bytes 2359296 | tf_op jit(solution)/shard_map/all_gather | solution.py:327
  24.5 287.3 %all-gather.11.cloned.1.call-start = ((), (), s32[]{:S(2)}) async-start(), calls=%async_computation.31 | async-start | bytes 14155776 | tf_op jit(solution)/shard_map/all_gather | solution.py:326
  32.4 329.0 %all-gather.17.cloned.1.call-start = ((), (), s32[]{:S(2)}) async-start(), calls=%async_computation.34 | async-start | bytes 2359296 | tf_op jit(solution)/shard_map/all_gather | solution.py:329
  40.0 379.6 %all-gather.19.cloned.1.call-start = ((), (), s32[]{:S(2)}) async-start(), calls=%async_computation.35 | async-start | bytes 2359296 | tf_op jit(solution)/shard_map/all_gather | solution.py:330
  47.0 438.2 %all-gather.21.cloned.1.call-start = ((), (), s32[]{:S(2)}) async-start(), calls=%async_computation.36 | async-start | bytes 4718592 | tf_op jit(solution)/shard_map/all_gather | solution.py:331
  334.4 30.2 %all-to-all-start.1 = ((bf16[256,4,256]{0,2,1:T(8,128)(2,1)}), bf16[256,4,256]{0,2,1:T(8,128)(2,1)S(1)}, u32[]{:S(2)}, u32[]{:S(2)}) async-start(bf16[256,4,256]{0,2,1:T(8,128)(2,1)} %bitcast.25), calls=%async_computation.1 | async-start | bytes 1048576 | tf_op jit(solution)/shard_map/all_to_all | solution.py:104
  364.5 18.3 %all-to-all-start.2 = ((bf16[256,4,256]{2,0,1:T(8,128)(2,1)}), bf16[256,4,256]{2,0,1:T(8,128)(2,1)S(1)}, u32[]{:S(2)}, u32[]{:S(2)}) async-start(bf16[256,4,256]{2,0,1:T(8,128)(2,1)} %bitcast.362), calls=%async_computation.2 | async-start | bytes 1048576 | tf_op jit(solution)/shard_map/all_to_all | solution.py:105
  368.0 191.0 %all-gather.23.cloned.1.call-start = ((), (), s32[]{:S(2)}) async-start(), calls=%async_computation.37 | async-start | bytes 4718592 | tf_op jit(solution)/shard_map/all_gather | solution.py:332
  790.1 164.0 %reduce-scatter.31.cloned.1.call-start = ((), (), s32[]{:S(2)}) async-start(), calls=%async_computation.46 | async-start | bytes 2621440 | tf_op jit(solution)/shard_map/reduce_scatter | solution.py:384
  877.9 76.7 %reduce-scatter.19.cloned.1.call-start = ((), (), s32[]{:S(2)}) async-start(), calls=%async_computation.40 | async-start | bytes 2621440 | tf_op jit(solution)/shard_map/reduce_scatter | solution.py:384
  891.6 63.6 %reduce-scatter.23.cloned.1.call-start = ((), (), s32[]{:S(2)}) async-start(), calls=%async_computation.42 | async-start | bytes 2621440 | tf_op jit(solution)/shard_map/reduce_scatter | solution.py:384
  900.4 88.2 %reduce-scatter.27.cloned.1.call-start = ((), (), s32[]{:S(2)}) async-start(), calls=%async_computation.44 | async-start | bytes 2621440 | tf_op jit(solution)/shard_map/reduce_scatter | solution.py:384
  915.2 120.4 %reduce-scatter.35.cloned.1.call-start = ((), (), s32[]{:S(2)}) async-start(), calls=%async_computation.48 | async-start | bytes 5242880 | tf_op jit(solution)/shard_map/reduce_scatter | solution.py:384
  921.7 161.0 %reduce-scatter.39.cloned.1.call-start = ((), (), s32[]{:S(2)}) async-start(), calls=%async_computation.50 | async-start | bytes 5242880 | tf_op jit(solution)/shard_map/reduce_scatter | solution.py:384
  930.3 254.0 %reduce-scatter.15.cloned.1.call-start = ((), (), s32[]{:S(2)}) async-start(), calls=%async_computation.38 | async-start | bytes 15728640 | tf_op jit(solution)/shard_map/reduce_scatter | solution.py:384
  954.0 295.5 %reduce-scatter.33.cloned.1.call-start = ((), (), s32[]{:S(2)}) async-start(), calls=%async_computation.47 | async-start | bytes 589824 | tf_op jit(solution)/shard_map/reduce_scatter | solution.py:390
  954.6 359.4 %reduce-scatter.21.cloned.1.call-start = ((), (), s32[]{:S(2)}) async-start(), calls=%async_computation.41 | async-start | bytes 589824 | tf_op jit(solution)/shard_map/reduce_scatter | solution.py:390
  955.2 423.0 %reduce-scatter.25.cloned.1.call-start = ((), (), s32[]{:S(2)}) async-start(), calls=%async_computation.43 | async-start | bytes 589824 | tf_op jit(solution)/shard_map/reduce_scatter | solution.py:390
  955.7 487.1 %reduce-scatter.29.cloned.1.call-start = ((), (), s32[]{:S(2)}) async-start(), calls=%async_computation.45 | async-start | bytes 589824 | tf_op jit(solution)/shard_map/reduce_scatter | solution.py:390
  988.6 519.8 %reduce-scatter.37.cloned.1.call-start = ((), (), s32[]{:S(2)}) async-start(), calls=%async_computation.49 | async-start | bytes 1179648 | tf_op jit(solution)/shard_map/reduce_scatter | solution.py:390
  1035.7 539.0 %reduce-scatter.41.cloned.1.call-start = ((), (), s32[]{:S(2)}) async-start(), calls=%async_computation.51 | async-start | bytes 1179648 | tf_op jit(solution)/shard_map/reduce_scatter | solution.py:390
  1082.8 569.0 %reduce-scatter.17.cloned.1.call-start = ((), (), s32[]{:S(2)}) async-start(), calls=%async_computation.39 | async-start | bytes 3538944 | tf_op jit(solution)/shard_map/reduce_scatter | solution.py:390
  (157 other events, 4806.0 us)
Sparse Core Ops, SparseCore 0:
  9.6 22.7 all-gather.8
  34.5 50.3 all-gather.14
  87.0 47.7 all-gather.12
  136.9 174.9 all-gather.10
  313.8 47.5 all-gather.16
  363.3 47.7 all-gather.18
  413.3 71.8 all-gather.20
  487.3 71.6 all-gather.22
  795.5 30.1 reduce-scatter.30
  891.7 29.8 reduce-scatter.18
  924.1 30.4 reduce-scatter.22
  957.2 31.3 reduce-scatter.26
  991.1 44.4 reduce-scatter.34
  1038.2 44.4 reduce-scatter.38
  1085.2 99.0 reduce-scatter.14
  1187.5 61.9 reduce-scatter.32
  1253.0 60.8 reduce-scatter.20
  1317.2 60.9 reduce-scatter.24
  1381.9 60.8 reduce-scatter.28
  1446.1 62.3 reduce-scatter.36
  1512.3 62.4 reduce-scatter.40
  1578.3 73.4 reduce-scatter.16
where the time goes:
time: 1670 us; the launch traced here: 1660 us
  waiting for transfers between devices  1150 us (69%)
  matrix products  234 us (14%)
  local copies, waits for them, and re-layouts  77.4 us (5%)
  other arithmetic  63 us (4%)
  starting transfers between devices  61.9 us (4%)
  blocking collectives  58.2 us (3%)
  between operations  16.7 us (1%)
    reduce_scatter x7, waiting for transfers between devices, local(): lax.psum_scatter(for_sending(col_sums), 'dp', scatter_dimension=0, tiled=...  433 us
    reduce_scatter x7, waiting for transfers between devices, local(): lax.psum_scatter(for_sending((ada_term,) + term_total), 'sp', scatter_dim...  228 us
    all_gather x1, waiting for transfers between devices, local(): lax.all_gather(columns[0], 'dp', axis=0, tiled=True)  173 us
    all_gather x1, waiting for transfers between devices, local(): lax.all_gather(columns[6], 'dp', axis=0, tiled=True)  68.6 us
    all_gather x1, waiting for transfers between devices, local(): lax.all_gather(columns[5], 'dp', axis=0, tiled=True)  60.7 us
    all_gather x1, waiting for transfers between devices, local(): lax.all_gather(columns[1], 'dp', axis=0, tiled=True)  47.1 us
  transfers between devices with their start and end apart: 38, of which 32 were waited for; matrix products, arithmetic and copies ran while one was open for 14% of the time, Pallas kernels for 0%

commit v1 on v0

v1 whole, which is shorter than its diff:
```python
import functools

import jax
import jax.numpy as jnp
from jax import lax
from jax.experimental import pallas as pl
from jax.experimental.pallas import tpu as pltpu
from jax.sharding import Mesh
from jax.sharding import PartitionSpec as P

HEAD_DIM = 64
PAIR = 2 * HEAD_DIM
LOG2E = 1.4426950408889634
LN2 = 0.6931471805599453
HIGH = lax.Precision.HIGHEST
F32 = jnp.float32
BF = jnp.bfloat16
NN = (((1,), (0,)), ((), ()))
NT = (((1,), (1,)), ((), ()))
TN = (((0,), (0,)), ((), ()))
ANY = pl.BlockSpec(memory_space=pl.ANY)
VM = pl.BlockSpec(memory_space=pltpu.VMEM)
MIB = 1 << 20


def dot(left, right, dims=NN):
    return lax.dot_general(left, right, dims, preferred_element_type=F32)


def sds(shape, dtype):
    return jax.ShapeDtypeStruct(shape, dtype)


def call(kernel, name, outs, in_specs, out_specs, args, grid=(), scratch=(), flops=0, vmem=40):
    moved = sum(x.size * x.dtype.itemsize for x in args)
    moved += sum(x.size * x.dtype.itemsize for x in outs)
    return pl.pallas_call(
        kernel,
        name=name,
        grid=grid,
        in_specs=in_specs,
        out_specs=out_specs,
        out_shape=outs,
        scratch_shapes=scratch,
        compiler_params=pltpu.CompilerParams(vmem_limit_bytes=vmem * MIB),
        cost_estimate=pl.CostEstimate(flops=flops, bytes_accessed=moved, transcendentals=0),
    )(*args)


def rows_of(block, width):
    return pl.BlockSpec((block, width), lambda i: (i, 0))


def fixed(*shape):
    return pl.BlockSpec(shape, lambda *_: (0,) * len(shape))


def swap(value, axis, offset=1):
    count = lax.axis_size(axis)
    return lax.ppermute(value, axis, [(i, i ^ offset) for i in range(count)])


def doubled(value, axes):
    for axis in axes:
        step = 1
        while step < lax.axis_size(axis):
            value = jnp.concatenate([value, swap(value, axis, step)], axis=0)
            step *= 2
    return value


def halved(value, axes):
    for axis in reversed(axes):
        step = lax.axis_size(axis) // 2
        while step:
            half = value.shape[0] // 2
            value = value[:half] + swap(value[half:], axis, step)
            step //= 2
    return value


def gather_blocks(shard):
    line = lax.axis_size("a")
    half = line // 2
    first = jnp.stack([shard] + [swap(shard, "a", d) for d in range(1, line)])
    blocks = {(0, 0): [(0, first)], (0, 1): [(0, swap(first, "r"))]}
    for dy in range(1, lax.axis_size("b")):
        blocks[(dy, 0)] = [(0, swap(first, "b", dy))]
    for dy in range(1, lax.axis_size("b")):
        blocks[(dy, 1)] = [
            (0, swap(blocks[(dy, 0)][0][1][:half], "r")),
            (half, swap(blocks[(0, 1)][0][1][half:], "b", dy)),
        ]
    return blocks


def scatter_blocks(parts):
    line = lax.axis_size("a")
    half = line // 2
    count_b = lax.axis_size("b")
    get = lambda dy, dr: sum(part[dy, dr].astype(F32) for part in parts)
    first_r = {}
    first_b = {}
    for dy in range(1, count_b):
        corner = get(dy, 1).astype(BF)
        first_r[dy] = swap(corner[:half], "r")
        first_b[dy] = swap(corner[half:], "b", dy)
    side = get(0, 1)
    extra = sum(part.astype(F32) for part in first_b.values())
    side = jnp.concatenate([side[:half], side[half:] + extra]).astype(BF)
    total = get(0, 0) + swap(side, "r").astype(F32)
    for dy in range(1, count_b):
        side = get(dy, 0)
        side = jnp.concatenate([side[:half] + first_r[dy].astype(F32), side[half:]]).astype(BF)
        total = total + swap(side, "b", dy).astype(F32)
    final = total[0]
    sent = total.astype(BF)
    for dz in range(1, line):
        final = final + swap(sent[dz], "a", dz).astype(F32)
    return final


def assemble_kernel(meta, keep_r, count_b, *refs):
    ins, out, sems = refs[: len(meta)], refs[len(meta)], refs[len(meta) + 1]
    at_a, at_b, at_r = (lax.axis_index(name) for name in ("a", "b", "r"))
    copies = []
    for ref, (dy, dr, dz0) in zip(ins, meta):
        depth = ref.shape[1]
        for t in range(ref.shape[0]):
            row = pl.multiple_of(((at_a ^ (dz0 + t)) * count_b + (at_b ^ dy)) * depth, depth)
            place = out.at[at_r ^ dr] if keep_r else out
            copy = pltpu.make_async_copy(
                ref.at[t], place.at[pl.ds(row, depth), :], sems.at[len(copies)]
            )
            copy.start()
            copies.append(copy)
    for copy in copies:
        copy.wait()


def assemble(blocks, rights, name):
    count_a, count_b = lax.axis_size("a"), lax.axis_size("b")
    arrays, meta = [], []
    for (dy, dr), pieces in blocks.items():
        if dr in rights:
            for dz0, piece in pieces:
                arrays.append(piece)
                meta.append((dy, dr, dz0))
    _, depth, width = arrays[0].shape
    keep_r = len(rights) > 1
    shape = (count_a * count_b * depth, width)
    if keep_r:
        shape = (len(rights),) + shape
    total = sum(x.shape[0] for x in arrays)
    return call(
        functools.partial(assemble_kernel, tuple(meta), keep_r, count_b),
        name,
        [sds(shape, BF)],
        [ANY] * len(arrays),
        [ANY],
        arrays,
        scratch=[pltpu.SemaphoreType.DMA((total,))],
    )[0]


def normed(values):
    centre = values - jnp.mean(values, axis=-1, keepdims=True)
    spread = lax.rsqrt(jnp.mean(centre * centre, axis=-1, keepdims=True) + 1e-06)
    return centre * spread, spread


def norm_back(grad, norm, spread):
    return spread * (
        grad
        - jnp.mean(grad, axis=-1, keepdims=True)
        - norm * jnp.mean(grad * norm, axis=-1, keepdims=True)
    )


def attn_input_kernel(x_ref, mod_ref, out_ref):
    norm, _ = normed(x_ref[...].astype(F32))
    out_ref[...] = (norm * (1.0 + mod_ref[1:2, :]) + mod_ref[0:1, :]).astype(BF)


def lane_ids(width=PAIR):
    return lax.broadcasted_iota(jnp.int32, (1, width), 1)


def turn(values, cosine, sine):
    early = lane_ids() % HEAD_DIM < HEAD_DIM // 2
    step = HEAD_DIM // 2
    other = jnp.where(early, pltpu.roll(values, PAIR - step, 1), pltpu.roll(values, step, 1))
    return values * cosine + other * sine


def qkv_kernel(x_ref, w_ref, cos_ref, sin_ref, q_ref, k_ref, v_ref):
    width = q_ref.shape[1]
    both = dot(x_ref[...], w_ref[...])
    cosine, sine = cos_ref[...], sin_ref[...]
    for lane in range(0, width, PAIR):
        q_ref[:, lane : lane + PAIR] = (
            turn(both[:, lane : lane + PAIR], cosine, sine) * (HEAD_DIM**-0.5 * LOG2E)
        ).astype(BF)
        at = width + lane
        k_ref[:, lane : lane + PAIR] = turn(both[:, at : at + PAIR], cosine, sine).astype(BF)
    v_ref[...] = both[:, 2 * width :].astype(BF)


def attend_kernel(block, q_ref, k_ref, v_ref, aq_ref, ak_ref, o_ref, lse_ref):
    frames = q_ref.shape[0]
    keys = jnp.concatenate([k_ref[...], ak_ref[...]], axis=1)
    values = v_ref[...]
    low = lane_ids() < HEAD_DIM
    zero, one = jnp.zeros((), BF), jnp.ones((), BF)

    def attend(with_max):
        for start in range(0, frames, block):
            rows = pl.ds(start, block)
            query, extra = q_ref[rows, :], aq_ref[rows, :]
            outs, logs = [], []
            for head in range(2):
                mine = low if head == 0 else jnp.logical_not(low)
                left = jnp.concatenate([jnp.where(mine, query, zero), extra], axis=1)
                scores = dot(left, keys, NT)
                if with_max:
                    top = jnp.max(scores, axis=1, keepdims=True)
                    scores = scores - top
                weights = jnp.exp2(scores).astype(BF)
                mixed = dot(weights, jnp.where(mine, values, one))
                outs.append(mixed / pltpu.roll(mixed, HEAD_DIM, 1))
                log = jnp.log2(jnp.maximum(mixed, 1e-30))
                logs.append(log + top if with_max else log)
            o_ref[rows, :] = jnp.where(low, outs[0], outs[1]).astype(BF)
            lse_ref[rows, :] = jnp.where(low, logs[1], logs[0])

    query_all, key_all = q_ref[...].astype(F32), k_ref[...].astype(F32)
    bound = jnp.max(jnp.sum(query_all * query_all, axis=1)) * jnp.max(
        jnp.sum(key_all * key_all, axis=1)
    )
    small = bound < 3600.0

    @pl.when(small)
    def _():
        attend(False)

    @pl.when(jnp.logical_not(small))
    def _():
        attend(True)


def split3(values):
    first = values.astype(BF)
    rest = values - first.astype(F32)
    second = rest.astype(BF)
    return first, second, (rest - second.astype(F32)).astype(BF)


def placed(parts, start, base):
    lanes = lane_ids()
    for i, part in enumerate(parts):
        base = jnp.where(lanes == start + i, part, base)
    return base


def attend_back_kernel(block, parts, q_ref, k_ref, v_ref, aq_ref, ak_ref, o_ref, lse_ref, cos_ref, sin_ref, *refs):
    do_refs, (dq_ref, dk_ref, dv_ref) = refs[:parts], refs[parts:]
    frames = q_ref.shape[0]
    lanes = lane_ids()
    low = lanes < HEAD_DIM
    zero = jnp.zeros((), BF)
    query, extra, lse = q_ref[...], aq_ref[...], lse_ref[...]
    grad = jnp.concatenate([ref[...] for ref in do_refs], axis=0)
    product = grad.astype(F32) * o_ref[...].astype(F32)
    queries, grads, lefts, rights = [], [], [], []
    for head in range(2):
        mine = low if head == 0 else jnp.logical_not(low)
        log = lse[:, HEAD_DIM : HEAD_DIM + 1] if head == 0 else lse[:, 0:1]
        queries.append(jnp.where(mine, query, zero))
        lefts.append(jnp.concatenate([queries[-1], placed(split3(-log), 8, extra)], axis=1))
        inner = -jnp.sum(jnp.where(mine, product, 0.0), axis=1, keepdims=True)
        grads.append(jnp.where(mine, grad, zero))
        tail = placed(split3(inner), 0, jnp.zeros((frames, PAIR), BF))
        rights.append(jnp.concatenate([grads[-1], tail], axis=1))
    ones = jnp.where(lanes < 3, 1.0, 0.0).astype(BF)
    dq_turned = jnp.zeros((PAIR, frames), F32)
    for start in range(0, frames, block):
        rows = pl.ds(start, block)
        key, value = k_ref[rows, :], v_ref[rows, :]
        keys = jnp.concatenate([key, ak_ref[rows, :]], axis=1)
        values = jnp.concatenate([value, jnp.broadcast_to(ones, value.shape)], axis=1)
        dv, dk = 0.0, 0.0
        for head in range(2):
            mine = low if head == 0 else jnp.logical_not(low)
            soft = jnp.exp2(dot(keys, lefts[head], NT))
            d_scores = (soft * dot(values, rights[head], NT)).astype(BF)
            dv = dv + dot(soft.astype(BF), grads[head])
            dk = dk + dot(d_scores, queries[head])
            dq_turned = dq_turned + dot(jnp.where(mine, key, zero), d_scores, TN)
        dv_ref[rows, :] = dv.astype(BF)
        dk_ref[rows, :] = turn(dk * LN2, cos_ref[rows, :], -sin_ref[rows, :]).astype(BF)
    dq = dq_turned.T * HEAD_DIM**-0.5
    dq_ref[...] = turn(dq, cos_ref[...], -sin_ref[...]).astype(BF)


def column(dr, dp):
    at_r, at_p = lax.axis_index("r"), lax.axis_index("p")
    return (at_r ^ dr) * lax.axis_size("p") + (at_p ^ dp)


def lanes_of(index, width):
    return pl.ds(pl.multiple_of(index * width, width), width)


def column_blocks(weight_refs):
    count_r = lax.axis_size("r")
    count_p = lax.axis_size("p")
    at_p = lax.axis_index("p")
    for dp, ref in enumerate(weight_refs):
        for r in range(count_r):
            yield r * count_p + (at_p ^ dp), ref, r


def out_kernel(count_p, x_ref, mod_ref, *refs):
    att_refs = refs[: 2 * count_p]
    w_refs = refs[2 * count_p : 3 * count_p]
    branch_ref, mid_ref, ffn_ref, att_ref, sum_ref = refs[3 * count_p :]
    width = att_refs[0].shape[1]
    for dp in range(count_p):
        for dr in range(2):
            att_ref[:, lanes_of(column(dr, dp), width)] = att_refs[2 * dp + dr][...]
    att = att_ref[...]
    for j, ref, r in column_blocks(w_refs):
        sum_ref[:, lanes_of(j, ref.shape[2])] = dot(att, ref[r])
    branch = sum_ref[...]
    branch_ref[...] = branch.astype(BF)
    mid = x_ref[...].astype(F32) + mod_ref[2:3, :] * branch
    mid_ref[...] = mid
    norm, _ = normed(mid)
    ffn_ref[...] = (norm * (1.0 + mod_ref[4:5, :]) + mod_ref[3:4, :]).astype(BF)


def up_kernel(count_p, x_ref, *refs):
    w_refs, (gelu_ref, slope_ref) = refs[:count_p], refs[count_p:]
    x = x_ref[...]
    root = 0.7978845608028654
    for j, ref, r in column_blocks(w_refs):
        up = dot(x, ref[r])
        square = up * up
        tanh = jnp.tanh(root * (up + 0.044715 * up * square))
        half = 0.5 * (1.0 + tanh)
        at = lanes_of(j, ref.shape[2])
        gelu_ref[:, at] = (up * half).astype(BF)
        slope = half + 0.5 * up * (1.0 - tanh * tanh) * (root * (1.0 + 0.134145 * square))
        slope_ref[:, at] = slope.astype(BF)


def down_kernel(count_p, gelu_ref, mid_ref, cot_ref, mod_ref, *refs):
    w_refs = refs[:count_p]
    out_ref, dbf_ref, dgate_ref, sum_ref = refs[count_p:]
    gelu = gelu_ref[...]
    for j, ref, r in column_blocks(w_refs):
        sum_ref[:, lanes_of(j, ref.shape[2])] = dot(gelu, ref[r])
    branch = sum_ref[...]
    gate = mod_ref[5:6, :]
    out_ref[...] = (mid_ref[...] + gate * branch).astype(BF)
    cot = cot_ref[...].astype(F32)
    dbf_ref[...] = (cot * gate).astype(BF)

    @pl.when(pl.program_id(0) == 0)
    def _():
        dgate_ref[...] = jnp.zeros_like(dgate_ref)

    dgate_ref[...] += jnp.sum(cot * branch, axis=0, keepdims=True)


def turned_dot(x_ref, w_refs):
    total = 0.0
    for j, ref, r in column_blocks(w_refs):
        total = total + dot(x_ref[:, lanes_of(j, ref.shape[2])], ref[r], NT)
    return total


def d_up_kernel(count_p, dbf_ref, slope_ref, *refs):
    w_refs, (out_ref,) = refs[:count_p], refs[count_p:]
    out_ref[...] = (turned_dot(dbf_ref, w_refs) * slope_ref[...].astype(F32)).astype(BF)


def mid_back_kernel(count_p, d_up_ref, mid_ref, cot_ref, branch_ref, mod_ref, *refs):
    up_refs, o_refs = refs[:count_p], refs[count_p : 2 * count_p]
    d_mid_ref, dba_ref, sums_ref = refs[2 * count_p : 2 * count_p + 3]
    att_refs, att_all = refs[2 * count_p + 3 : -1], refs[-1]
    d_in = turned_dot(d_up_ref, up_refs)
    norm, spread = normed(mid_ref[...])

    @pl.when(pl.program_id(0) == 0)
    def _():
        sums_ref[...] = jnp.zeros_like(sums_ref)

    sums_ref[1:2, :] += jnp.sum(d_in, axis=0, keepdims=True)
    sums_ref[2:3, :] += jnp.sum(d_in * norm, axis=0, keepdims=True)
    d_mid = cot_ref[...].astype(F32) + norm_back(d_in * (1.0 + mod_ref[4:5, :]), norm, spread)
    d_mid_ref[...] = d_mid
    sums_ref[0:1, :] += jnp.sum(d_mid * branch_ref[...].astype(F32), axis=0, keepdims=True)
    dba_ref[...] = (d_mid * mod_ref[2:3, :]).astype(BF)
    att_all[...] = turned_dot(dba_ref, o_refs)
    for dp in range(count_p):
        for dr in range(2):
            ref = att_refs[2 * dp + dr]
            ref[...] = att_all[:, lanes_of(column(dr, dp), ref.shape[1])].astype(BF)


def weight_grad_kernel(count_x, places, sizes, count_y, *refs):
    x_refs, y_refs = refs[:count_x], refs[count_x : count_x + count_y]
    out_refs = refs[count_x + count_y : -2]
    held, sems = refs[-2:]
    count_a, count_b = sizes
    at_a, at_b = lax.axis_index("a"), lax.axis_index("b")
    depth, width = out_refs[0].shape[-2:]
    x = x_refs[0][...] if count_x == 1 else jnp.concatenate([ref[...] for ref in x_refs], axis=1)
    copies = []
    for slot, (dp, dr) in enumerate(places):
        if dr is None:
            for t, ref in enumerate(y_refs):
                part = ref.shape[1]
                held[slot, :, t * part : (t + 1) * part] = dot(x, ref[...], TN).astype(BF)
        else:
            held[slot] = dot(x, y_refs[0][:, lanes_of(column(dr, dp), width)], TN).astype(BF)
        for dy in range(count_b):
            for dz in range(count_a):
                row = pl.multiple_of(((at_a ^ dz) * count_b + (at_b ^ dy)) * depth, depth)
                place = out_refs[dp].at[dy, dz] if dr is None else out_refs[dp].at[dy, dr, dz]
                copy = pltpu.make_async_copy(
                    held.at[slot, pl.ds(row, depth), :], place, sems.at[len(copies)]
                )
                copy.start()
                copies.append(copy)
    for copy in copies:
        copy.wait()


def weight_grad(name, x, ys, split):
    count_a, count_b = lax.axis_size("a"), lax.axis_size("b")
    count_p = lax.axis_size("p") if split else 1
    depth = x.shape[1] // (count_a * count_b)
    width = sum(y.shape[1] for y in ys)
    if split:
        width //= 2 * count_p
        places = [(dp, dr) for dp in reversed(range(count_p)) for dr in reversed(range(2))]
        outs = [sds((count_b, 2, count_a, depth, width), BF)] * count_p
    else:
        places = [(0, None)]
        outs = [sds((count_b, count_a, depth, width), BF)]
    return call(
        functools.partial(weight_grad_kernel, 1, tuple(places), (count_a, count_b), len(ys)),
        name,
        outs,
        [VM] * (1 + len(ys)),
        [ANY] * count_p,
        [x, *ys],
        scratch=[
            pltpu.VMEM((len(places), x.shape[1], width), BF),
            pltpu.SemaphoreType.DMA((len(places) * count_a * count_b,)),
        ],
        flops=2 * x.size * sum(y.shape[1] for y in ys),
    )


def qkv_turned(refs, ws):
    total = 0.0
    for t, ref in enumerate(refs):
        width = ref.shape[1]
        at = (t % 3) * width
        total = total + dot(ref[...], ws[t // 3][:, at : at + width], NT)
    return total


def d_attn_send_kernel(*refs):
    refs[-1][...] = qkv_turned(refs[:6], refs[6:8]).astype(BF)


def hidden_back_kernel(count_recv, *refs):
    d_refs, ws = refs[:6], refs[6:8]
    recv = refs[8 : 8 + count_recv]
    x_ref, d_mid_ref, mod_ref, out_ref, sums_ref = refs[8 + count_recv :]
    d_in = qkv_turned(d_refs, ws)
    for ref in recv:
        d_in = d_in + ref[...].astype(F32)
    norm, spread = normed(x_ref[...].astype(F32))

    @pl.when(pl.program_id(0) == 0)
    def _():
        sums_ref[...] = jnp.zeros_like(sums_ref)

    sums_ref[0:1, :] += jnp.sum(d_in, axis=0, keepdims=True)
    sums_ref[1:2, :] += jnp.sum(d_in * norm, axis=0, keepdims=True)
    back = norm_back(d_in * (1.0 + mod_ref[1:2, :]), norm, spread)
    out_ref[...] = (d_mid_ref[...] + back).astype(BF)


def exchange_rows(rows):
    at_r = lax.axis_index("r")
    own = lax.dynamic_index_in_dim(rows, at_r, keepdims=False)
    other = swap(lax.dynamic_index_in_dim(rows, 1 - at_r, keepdims=False), "r")
    return jnp.concatenate([own, other], axis=0)


def restore_rows(frames):
    half = frames.shape[0] // 2
    own, other = frames[:half], swap(frames[half:], "r")
    return jnp.where(lax.axis_index("r") == 0, jnp.stack([own, other]), jnp.stack([other, own]))


def by_columns(parts):
    count = parts.shape[0]
    me = lax.axis_index("r") * lax.axis_size("p") + lax.axis_index("p")
    step = 1
    while step < count:
        shape = (count // (2 * step), 2, step) + parts.shape[1:]
        grouped = parts.reshape(shape)
        flipped = jnp.flip(grouped, axis=1)
        parts = jnp.where((me & step) != 0, flipped, grouped).reshape(parts.shape)
        step *= 2
    return parts


def local(
    hidden_in,
    time_embed,
    seg_lengths,
    ada_weight,
    query_weight,
    key_weight,
    value_weight,
    out_weight,
    up_weight,
    down_weight,
    out_cotangent,
):
    count_a, count_b, count_p = (lax.axis_size(name) for name in ("a", "b", "p"))
    at_a, at_b, at_r, at_p = (lax.axis_index(name) for name in ("a", "b", "r", "p"))
    width = hidden_in.shape[2]
    block = hidden_in.shape[1]
    mine = 2 * block
    frames = mine * count_p
    heads_wide = query_weight.shape[1]
    ffn = up_weight.shape[1] * 2 * count_p
    others = range(1, count_p)

    qkv_blocks = gather_blocks(jnp.concatenate([query_weight, key_weight, value_weight], axis=1))
    hidden = exchange_rows(hidden_in)
    hidden_all = jnp.concatenate([hidden] + [swap(hidden, "p", dp) for dp in others], axis=0)

    time_vecs = time_embed.astype(F32)
    time_low = jax.nn.silu(time_vecs).astype(BF)
    low_all = doubled(time_low, ("b", "a"))
    ada_rows = ada_weight.shape[0]
    low_mine = lax.dynamic_slice_in_dim(
        low_all, (at_a * count_b + at_b) * ada_rows, ada_rows, axis=1
    )
    part = jnp.dot(low_mine, ada_weight, preferred_element_type=F32)
    part = halved(part, ("b", "a"))
    part = jnp.stack(
        [
            lax.dynamic_index_in_dim(part, at_r, keepdims=False),
            swap(lax.dynamic_index_in_dim(part, 1 - at_r, keepdims=False), "r"),
        ]
    )
    parts = [part] + [swap(part, "p", dp) for dp in others]
    parts = jnp.stack(parts, axis=1).reshape(2 * count_p, -1)
    modulation = by_columns(parts).reshape(6, width)

    lengths = lax.dynamic_index_in_dim(seg_lengths, at_r, keepdims=False)
    frame_ids = jnp.concatenate(
        [
            ((at_r ^ dr) * count_p + (at_p ^ dp)) * block + jnp.arange(block, dtype=jnp.int32)
            for dp in range(count_p)
            for dr in range(2)
        ]
    )
    passed = frame_ids[:, None] >= jnp.cumsum(lengths)[None, :]
    seg_ids = jnp.sum(passed.astype(jnp.int32), axis=1)
    positions = frame_ids - jnp.sum(jnp.where(passed, lengths[None, :], 0), axis=1)
    half_dim = HEAD_DIM // 2
    lane = jnp.arange(PAIR, dtype=jnp.int32)
    inverse = 10000.0 ** (-(lane % half_dim).astype(F32) / half_dim)
    angles = positions.astype(F32)[:, None] * inverse[None, :]
    cosine = jnp.cos(angles)
    sine = jnp.where(lane % HEAD_DIM < half_dim, -1.0, 1.0)[None, :] * jnp.sin(angles)
    segs = seg_lengths.shape[1]
    same = seg_ids[:, None] == lane[None, :]
    real = (lane < segs)[None, :]
    extra_q = jnp.where(real & ~same, -1e30, 0.0).astype(BF)
    extra_k = jnp.where((real & same) | ((lane >= 8) & (lane < 11))[None, :], 1.0, 0.0).astype(BF)

    tile = 256
    grid = (frames // tile,)
    attn_input = call(
        attn_input_kernel,
        "attn_input",
        [sds((frames, width), BF)],
        [rows_of(tile, width), fixed(6, width)],
        [rows_of(tile, width)],
        [hidden_all, modulation],
        grid=grid,
    )[0]

    q_w = [assemble(qkv_blocks, (dr,), "assemble_qkv") for dr in range(2)]
    pair_block = pl.BlockSpec((frames, PAIR), lambda i: (0, i))
    pair_fixed = fixed(frames, PAIR)
    qkv, attended = [], []
    for dr in range(2):
        heads = sds((frames, heads_wide), BF)
        qkv.append(
            call(
                qkv_kernel,
                "qkv",
                [heads] * 3,
                [rows_of(tile, width), fixed(width, 3 * heads_wide)] + [rows_of(tile, PAIR)] * 2,
                [rows_of(tile, heads_wide)] * 3,
                [attn_input, q_w[dr], cosine, sine],
                grid=grid,
                flops=6 * frames * width * heads_wide,
            )
        )
        attended.append(
            call(
                functools.partial(attend_kernel, min(256, frames)),
                "attend",
                [heads, sds((frames, heads_wide), F32)],
                [pair_block] * 3 + [pair_fixed] * 2,
                [pair_block] * 2,
                [*qkv[dr], extra_q, extra_k],
                grid=(heads_wide // PAIR,),
                flops=frames * frames * heads_wide * 16,
            )
        )

    def with_others(blocks, name):
        whole = assemble(blocks, (0, 1), name)
        return [whole] + [swap(whole, "p", dp) for dp in others]

    out_w = with_others(gather_blocks(out_weight), "assemble_out")
    up_w = with_others(gather_blocks(up_weight), "assemble_up")
    down_w = with_others(gather_blocks(down_weight), "assemble_down")
    cotangent = exchange_rows(out_cotangent)

    att = [attended[dr][0][:mine] for dr in range(2)]
    for dp in others:
        att += [swap(attended[dr][0][dp * mine : (dp + 1) * mine], "p", dp) for dr in range(2)]
    tile = min(256, mine)
    grid = (mine // tile,)
    full = rows_of(tile, width)
    wide = rows_of(tile, ffn)
    mod_spec = fixed(6, width)
    out_specs = [fixed(*w.shape) for w in out_w]
    up_specs = [fixed(*w.shape) for w in up_w]
    down_specs = [fixed(*w.shape) for w in down_w]
    branch_attn, mid, ffn_input = call(
        functools.partial(out_kernel, count_p),
        "attn_out",
        [sds((mine, width), BF), sds((mine, width), F32), sds((mine, width), BF)],
        [full, mod_spec] + [rows_of(tile, heads_wide)] * (2 * count_p) + out_specs,
        [full] * 3,
        [hidden, modulation, *att, *out_w],
        grid=grid,
        scratch=[pltpu.VMEM((tile, width), BF), pltpu.VMEM((tile, width), F32)],
        flops=2 * mine * width * width,
    )
    gelu_low, slope = call(
        functools.partial(up_kernel, count_p),
        "ffn_up",
        [sds((mine, ffn), BF)] * 2,
        [full] + up_specs,
        [wide] * 2,
        [ffn_input, *up_w],
        grid=grid,
        flops=2 * mine * width * ffn,
    )
    hidden_out, d_branch_ffn, d_ffn_gate = call(
        functools.partial(down_kernel, count_p),
        "ffn_down",
        [sds((mine, width), BF), sds((mine, width), BF), sds((1, width), F32)],
        [wide, full, full, mod_spec] + down_specs,
        [full, full, fixed(1, width)],
        [gelu_low, mid, cotangent, modulation, *down_w],
        grid=grid,
        scratch=[pltpu.VMEM((tile, width), F32)],
        flops=2 * mine * width * ffn,
    )
    hidden_out = restore_rows(hidden_out)

    def reduce_split(parts):
        own = [parts[0]] + [swap(parts[dp], "p", dp) for dp in others]
        return scatter_blocks(own)

    down_grad = reduce_split(weight_grad("down_grad", gelu_low, [d_branch_ffn], True))
    d_up = call(
        functools.partial(d_up_kernel, count_p),
        "d_up",
        [sds((mine, ffn), BF)],
        [full, wide] + down_specs,
        [wide],
        [d_branch_ffn, slope, *down_w],
        grid=grid,
        flops=2 * mine * width * ffn,
    )[0]
    up_grad = reduce_split(weight_grad("up_grad", ffn_input, [d_up], True))
    d_mid, d_branch_attn, sums_mid, *d_att = call(
        functools.partial(mid_back_kernel, count_p),
        "mid_back",
        [sds((mine, width), F32), sds((mine, width), BF), sds((3, width), F32)]
        + [sds((mine, heads_wide), BF)] * (2 * count_p),
        [wide, full, full, full, mod_spec] + up_specs + out_specs,
        [full, full, fixed(3, width)] + [rows_of(tile, heads_wide)] * (2 * count_p),
        [d_up, mid, cotangent, branch_attn, modulation, *up_w, *out_w],
        grid=grid,
        scratch=[pltpu.VMEM((tile, width), F32)],
        flops=2 * mine * width * (ffn + width),
    )
    att_all = [att[2 * dp + dr] for dp in range(count_p) for dr in range(2)]
    att_cols = by_columns(jnp.stack([att_all[2 * dp + dr] for dr in range(2) for dp in range(count_p)]))
    att_full = jnp.moveaxis(att_cols, 0, 1).reshape(mine, width)
    out_grad = reduce_split(weight_grad("out_grad", att_full, [d_branch_attn], True))

    d_qkv = [None, None]
    qkv_final = [None, None]
    grad_parts = [None, None]
    for dr in (1, 0):
        d_heads = [d_att[dr]] + [swap(d_att[2 * dp + dr], "p", dp) for dp in others]
        d_qkv[dr] = call(
            functools.partial(attend_back_kernel, min(512, frames), count_p),
            "attend_back",
            [sds((frames, heads_wide), BF)] * 3,
            [pair_block] * 3
            + [pair_fixed] * 2
            + [pair_block] * 2
            + [pair_fixed] * 2
            + [pl.BlockSpec((mine, PAIR), lambda i: (0, i))] * count_p,
            [pair_block] * 3,
            [*qkv[dr], extra_q, extra_k, *attended[dr], cosine, sine, *d_heads],
            grid=(heads_wide // PAIR,),
            flops=frames * frames * heads_wide * 40,
            vmem=56,
        )
        grad_parts[dr] = weight_grad("qkv_grad", attn_input, d_qkv[dr], False)[0]
    both = jnp.stack(grad_parts, axis=1)
    qkv_grad = scatter_blocks([both])

    six = [*d_qkv[0], *d_qkv[1]]
    w_specs = [fixed(width, 3 * heads_wide)] * 2
    received = []
    for dp in others:
        first = dp * mine // tile
        part_spec = pl.BlockSpec((tile, heads_wide), lambda i, first=first: (i + first, 0))
        sent = call(
            d_attn_send_kernel,
            "d_attn_send",
            [sds((mine, width), BF)],
            [part_spec] * 6 + w_specs,
            [full],
            [*six, *q_w],
            grid=grid,
            flops=12 * mine * width * heads_wide,
        )[0]
        received.append(swap(sent, "p", dp))
    hidden_grad, sums_in = call(
        functools.partial(hidden_back_kernel, len(received)),
        "hidden_back",
        [sds((mine, width), BF), sds((2, width), F32)],
        [rows_of(tile, heads_wide)] * 6 + w_specs + [full] * len(received) + [full, full, mod_spec],
        [full, fixed(2, width)],
        [*six, *q_w, *received, hidden, d_mid, modulation],
        grid=grid,
        flops=12 * mine * width * heads_wide,
    )
    hidden_grad = restore_rows(hidden_grad)

    d_mod = jnp.concatenate([sums_in, sums_mid, d_ffn_gate], axis=0).reshape(2, count_p, -1)
    d_cols = lax.dynamic_index_in_dim(d_mod, at_p, axis=1, keepdims=False)
    for dp in others:
        d_cols = d_cols + swap(
            lax.dynamic_index_in_dim(d_mod, at_p ^ dp, axis=1, keepdims=False), "p", dp
        )
    own = lax.dynamic_index_in_dim(d_cols, at_r, keepdims=False)
    other = swap(lax.dynamic_index_in_dim(d_cols, 1 - at_r, keepdims=False), "r")
    d_rows = jnp.where(at_r == 0, jnp.stack([own, other]), jnp.stack([other, own]))
    d_rows = doubled(d_rows, ("b", "a"))
    ada_grad = jnp.dot(low_mine.astype(F32).T, d_rows, precision=HIGH)
    d_low = jnp.dot(d_rows, ada_weight.astype(F32).T, precision=HIGH)
    d_low = d_low + swap(d_low, "r")
    step = 1
    while step < count_p:
        d_low = d_low + swap(d_low, "p", step)
        step *= 2
    spread = jnp.zeros((d_low.shape[0], width), F32)
    spread = lax.dynamic_update_slice_in_dim(
        spread, d_low, (at_a * count_b + at_b) * ada_rows, axis=1
    )
    d_time_low = halved(spread, ("b", "a"))
    _, silu_pullback = jax.vjp(jax.nn.silu, time_vecs)
    time_grad = silu_pullback(d_time_low)[0]

    return (
        hidden_out,
        hidden_grad,
        time_grad,
        ada_grad,
        qkv_grad[:, :heads_wide],
        qkv_grad[:, heads_wide : 2 * heads_wide],
        qkv_grad[:, 2 * heads_wide :],
        out_grad,
        up_grad,
        down_grad,
    )


def solution(mesh):
    count_dp, count_sp = mesh.shape["dp"], mesh.shape["sp"]
    fine = Mesh(mesh.devices.reshape(4, count_dp // 4, 2, count_sp // 2), ("a", "b", "r", "p"))
    dp, sp = ("a", "b"), ("r", "p")
    in_specs = (
        (P(dp, sp, None), P(dp, None), P(dp, None)) + (P(dp, sp),) * 7 + (P(dp, sp, None),)
    )
    out_specs = (P(dp, sp, None), P(dp, sp, None), P(dp, None)) + (P(dp, sp),) * 7
    return jax.shard_map(local, mesh=fine, in_specs=in_specs, out_specs=out_specs, check_vma=False)
```

time: 1670 us -> 469 us (0.28)
  waiting for transfers between devices: 1150 us -> 122 us
  matrix products: 234 us -> 2.09 us
  Pallas kernels: 0 us -> 149 us
  blocking collectives: 58.2 us -> 0 us
  starting transfers between devices: 61.9 us -> 103 us
  local copies, waits for them, and re-layouts: 77.4 us -> 47 us
  other arithmetic: 63 us -> 35.6 us
    reduce_scatter x14 -> x0, waiting for transfers between devices: 661 us -> none  [the longest x7 433 us: local(): lax.psum_scatter(for_sending(col_sums), 'dp', scatter_dimension=0, tiled=...]
    all_gather x8 -> x0, waiting for transfers between devices: 408 us -> none  [the longest x1 173 us: local(): lax.all_gather(columns[0], 'dp', axis=0, tiled=True)]
    dot_general x68 -> x3, matrix products: 234 us -> 2.09 us  [the longest x1 1.48 us: local(): ada_grad = jnp.dot(low_mine.astype(F32).T, d_rows, precision=HIGH)]
    pallas_call x0 -> x24, Pallas kernels: none -> 149 us  [call(): pl.pallas_call(kernel, name=name, grid=grid, in_specs=in_specs, out_specs...]
    ppermute x0 -> x90, waiting for transfers between devices: none -> 122 us  [swap(): return lax.ppermute(value, axis, [(i, i ^ offset) for i in range(count)])]
    ppermute x0 -> x90, starting transfers between devices: none -> 103 us  [swap(): return lax.ppermute(value, axis, [(i, i ^ offset) for i in range(count)])]
    all_to_all x16 -> x0, waiting for transfers between devices: 77.6 us -> none  [the longest x2 15.9 us: forward_row(): lax.all_to_all(query_rot, 'sp', split_axis=1, concat_axis=0, tiled=True)]
    all_to_all x16 -> x0, starting transfers between devices: 60 us -> none  [the longest x2 8.67 us: backward_row(): lax.all_to_all(d_attended, 'sp', split_axis=1, concat_axis=0, tiled=True)]
  transfers between devices with their start and end apart: 38 -> 90, of which waited for: 32 -> 34; matrix products, arithmetic and copies ran while one was open for 14% -> 13% of each run, Pallas kernels for 0% -> 31%
where the time goes in v1:
time: 469 us; the launch traced here: 461 us
  Pallas kernels  149 us (32%)
  waiting for transfers between devices  122 us (26%)
  starting transfers between devices  103 us (22%)
  local copies, waits for them, and re-layouts  47 us (10%)
  other arithmetic  35.6 us (8%)
    pallas_call x24, Pallas kernels, call(): pl.pallas_call(kernel, name=name, grid=grid, in_specs=in_specs, out_specs...  149 us
    ppermute x90, waiting for transfers between devices, swap(): return lax.ppermute(value, axis, [(i, i ^ offset) for i in range(count)])  122 us
    ppermute x90, starting transfers between devices, swap(): return lax.ppermute(value, axis, [(i, i ^ offset) for i in range(count)])  103 us
    unnamed x222, local copies, waits for them, and re-layouts  22.7 us
  transfers between devices with their start and end apart: 90, of which 34 were waited for; matrix products, arithmetic and copies ran while one was open for 13% of the time, Pallas kernels for 31%

profile of v1, /device:TPU:0, one launch (start us, length us, event | category | flops | bytes accessed | tf_op | source)
XLA Modules:
  0.0 461.2 jit_solution(9904054037051747941)
XLA Ops:
  0.7 5.1 %collective-permute-start.21 = (bf16[128,256]{1,0:T(8,128)(2,1)}, bf16[128,256]{1,0:T(8,128)(2,1)S(1)}, u32[]{:S(2)}, u32[]{:S(2)}) collective-permute-start(bf16[128,256]{1,0:T(8,128)(2,1)} %param.18), channel_id=1, source_target_pairs={{0,24},{8,16},{16,8},{24,0},{1,25},{9,17},{17,9},{25,1},{2,26},{10... | collective-permute-start | bytes 196616 | tf_op jit(solution)/shard_map/ppermute | solution.py:60
  45.2 8.6 %collective-permute-done.28 = bf16[128,512]{1,0:T(8,128)(2,1)S(1)} collective-permute-done((bf16[128,512]{1,0:T(8,128)(2,1)S(1)}, bf16[128,512]{1,0:T(8,128)(2,1)S(1)}, u32[]{:S(2)}, u32[]{:S(2)}) %collective-permute-start.28) | collective-permute-done | bytes 131104 | tf_op jit(solution)/shard_map/ppermute | solution.py:60
  55.6 6.1 %collective-permute-done.37 = bf16[256,256]{1,0:T(8,128)(2,1)S(1)} collective-permute-done((bf16[256,256]{1,0:T(8,128)(2,1)S(1)}, bf16[256,256]{1,0:T(8,128)(2,1)S(1)}, u32[]{:S(2)}, u32[]{:S(2)}) %collective-permute-start.37) | collective-permute-done | bytes 131104 | tf_op jit(solution)/shard_map/ppermute | solution.py:60
  71.4 8.2 %collective-permute-done.22.refs_1_ = bf16[4,128,256]{2,1,0:T(8,128)(2,1)S(1)} collective-permute-done((bf16[4,128,256]{2,1,0:T(8,128)(2,1)S(1)}, bf16[4,128,256]{2,1,0:T(8,128)(2,1)S(1)}, u32[]{:S(2)}, u32[]{:S(2)}) %collective-permute-start.22) | collective-permute-done | bytes 262176 | tf_op jit(solution)/shard_map/ppermute | solution.py:60
  94.5 14.5 %collective-permute-done.39.refs_1_ = bf16[4,256,256]{2,1,0:T(8,128)(2,1)} collective-permute-done((bf16[4,256,256]{2,1,0:T(8,128)(2,1)S(1)}, bf16[4,256,256]{2,1,0:T(8,128)(2,1)}, u32[]{:S(2)}, u32[]{:S(2)}) %collective-permute-start.39) | collective-permute-done | bytes 524320 | tf_op jit(solution)/shard_map/ppermute | solution.py:60
  132.7 5.2 %assemble_out.1.refs_4_.refs_2_ = bf16[2,1024,256]{2,1,0:T(8,128)(2,1)} custom-call(bf16[4,128,256]{2,1,0:T(8,128)(2,1)S(1)} %pad_maximum_fusion.13.refs_0_, bf16[4,128,256]{2,1,0:T(8,128)(2,1)S(1)} %copy-done.49, bf16[4,128,256]{2,1,0:T(8,128)(2,1)S(1)} %copy-done.52, bf16[2,128,256]{2,1,0:T(8,128)(2,1)} %collective-permute-done.24.refs_3_, ...), custom_call_target="tpu_custom_call" | custom-call | bytes 2097152 | tf_op jit(solution)/shard_map/assemble_out/pallas_call | solution.py:37
  137.9 17.2 %assemble_up.1.refs_0_ = bf16[2,1024,512]{2,1,0:T(8,128)(2,1)} custom-call(bf16[4,128,512]{2,1,0:T(8,128)(2,1)S(1)} %pad_maximum_fusion.7.refs_0_, bf16[4,128,512]{2,1,0:T(8,128)(2,1)S(1)} %copy-done.37, bf16[4,128,512]{2,1,0:T(8,128)(2,1)} %collective-permute-done.31.refs_2_, bf16[2,128,512]{2,1,0:T(8,128)(2,1)S(1)} %collective-permute-done.32.refs_3_, ...), custom_call_target="tpu_custom_call" | custom-call | bytes 4194304 | tf_op jit(solution)/shard_map/assemble_up/pallas_call | solution.py:37
  170.0 8.5 %attend.2 = (bf16[1024,256]{1,0:T(8,128)(2,1)S(1)}, f32[1024,256]{1,0:T(8,128)S(1)}) custom-call(bf16[1024,256]{1,0:T(8,128)(2,1)S(1)} %get-tuple-element.49.q_ref, bf16[1024,256]{1,0:T(8,128)(2,1)S(1)} %get-tuple-element.50.k_ref, bf16[1024,256]{1,0:T(8,128)(2,1)S(1)} %get-tuple-element.51.v_ref, bf16[1024,128]{1,0:T(8,128)(2,1)S(1)} %copy-done.60, ...), custom_call_target="tpu_custom_call" | custom-call | flops 4294967296 | bytes 3670016 | tf_op jit(solution)/shard_map/attend/pallas_call | solution.py:37
  181.5 8.7 %attend.3 = (bf16[1024,256]{1,0:T(8,128)(2,1)S(1)}, f32[1024,256]{1,0:T(8,128)S(1)}) custom-call(bf16[1024,256]{1,0:T(8,128)(2,1)S(1)} %get-tuple-element.53.q_ref, bf16[1024,256]{1,0:T(8,128)(2,1)S(1)} %get-tuple-element.54.k_ref, bf16[1024,256]{1,0:T(8,128)(2,1)S(1)} %get-tuple-element.55.v_ref, bf16[1024,128]{1,0:T(8,128)(2,1)S(1)} %copy-done.60, ...), custom_call_target="tpu_custom_call" | custom-call | flops 4294967296 | bytes 3670016 | tf_op jit(solution)/shard_map/attend/pallas_call | solution.py:37
  198.8 4.2 attn_out.1
  204.0 6.6 %ffn_up.1 = (bf16[512,2048]{1,0:T(8,128)(2,1)S(1)}, bf16[512,2048]{1,0:T(8,128)(2,1)S(1)}) custom-call(bf16[512,1024]{1,0:T(8,128)(2,1)S(1)} %get-tuple-element.57.x_ref.refs_0_, bf16[2,1024,512]{2,1,0:T(8,128)(2,1)} %assemble_up.1.refs_0_, bf16[2,1024,512]{2,1,0:T(8,128)(2,1)} %collective-permute-done.34.refs_1_), custom_call_target="tpu_custom_call" | custom-call | flops 2147483648 | bytes 9437184 | tf_op jit(solution)/shard_map/ffn_up/pallas_call | solution.py:37
  210.6 6.0 %ffn_down.1 = (bf16[512,1024]{1,0:T(8,128)(2,1)S(1)}, bf16[512,1024]{1,0:T(8,128)(2,1)S(1)}, f32[1,1024]{1,0:T(1,128)S(1)}) custom-call(bf16[512,2048]{1,0:T(8,128)(2,1)S(1)} %get-tuple-element.58.gelu_ref.refs_0_, f32[512,1024]{1,0:T(8,128)S(1)} %get-tuple-element.59.mid_ref, bf16[512,1024]{1,0:T(8,128)(2,1)S(1)} %pad_maximum_fusion.2.cot_ref, ...), custom_call_target="tpu_custom_call" | custom-call | flops 2147483648 | bytes 11563008 | tf_op jit(solution)/shard_map/ffn_down/pallas_call | solution.py:37
  218.6 4.2 d_up.1.d_up_ref.refs_1_
  222.8 6.1 %up_grad.1 = (bf16[2,2,4,128,512]{4,3,2,1,0:T(8,128)(2,1)S(1)}, bf16[2,2,4,128,512]{4,3,2,1,0:T(8,128)(2,1)}) custom-call(bf16[512,1024]{1,0:T(8,128)(2,1)S(1)} %get-tuple-element.57.x_ref.refs_0_, bf16[512,2048]{1,0:T(8,128)(2,1)S(1)} %d_up.1.d_up_ref.refs_1_), custom_call_target="tpu_custom_call" | custom-call | flops 2147483648 | bytes 7340032 | tf_op jit(solution)/shard_map/up_grad/pallas_call | solution.py:37
  230.4 9.4 %mid_back.1 = (f32[512,1024]{1,0:T(8,128)S(1)}, bf16[512,1024]{1,0:T(8,128)(2,1)S(1)}, f32[3,1024]{1,0:T(4,128)S(1)}, bf16[512,256]{1,0:T(8,128)(2,1)S(1)}, bf16...) custom-call(bf16[512,2048]{1,0:T(8,128)(2,1)S(1)} %d_up.1.d_up_ref.refs_1_, ...), custom_call_target="tpu_custom_call" | custom-call | flops 3221225472 | bytes 16814080 | tf_op jit(solution)/shard_map/mid_back/pallas_call | solution.py:37
  245.6 10.9 %down_grad.1 = (bf16[2,2,4,256,256]{4,3,2,1,0:T(8,128)(2,1)S(1)}, bf16[2,2,4,256,256]{4,3,2,1,0:T(8,128)(2,1)S(1)}) custom-call(bf16[512,2048]{1,0:T(8,128)(2,1)S(1)} %get-tuple-element.58.gelu_ref.refs_0_, bf16[512,1024]{1,0:T(8,128)(2,1)S(1)} %get-tuple-element.62.dbf_ref.refs_1_), custom_call_target="tpu_custom_call" | custom-call | flops 2147483648 | bytes 7340032 | tf_op jit(solution)/shard_map/down_grad/pallas_call | solution.py:37
  259.9 14.9 %attend_back.3 = (bf16[1024,256]{1,0:T(8,128)(2,1)}, bf16[1024,256]{1,0:T(8,128)(2,1)}, bf16[1024,256]{1,0:T(8,128)(2,1)}) custom-call(bf16[1024,256]{1,0:T(8,128)(2,1)} %copy-done.70, bf16[1024,256]{1,0:T(8,128)(2,1)} %copy-done.71, bf16[1024,256]{1,0:T(8,128)(2,1)} %copy-done.72, bf16[1024,128]{1,0:T(8,128)(2,1)} %get-tuple-element.154.aq_ref, ...), custom_call_target="tpu_custom_call" | custom-call | flops 10737418240 | bytes 6815744 | tf_op jit(solution)/shard_map/attend_back/pallas_call | solution.py:37
  285.0 15.4 %attend_back.2 = (bf16[1024,256]{1,0:T(8,128)(2,1)}, bf16[1024,256]{1,0:T(8,128)(2,1)}, bf16[1024,256]{1,0:T(8,128)(2,1)}) custom-call(bf16[1024,256]{1,0:T(8,128)(2,1)} %copy-done.67, bf16[1024,256]{1,0:T(8,128)(2,1)} %copy-done.68, bf16[1024,256]{1,0:T(8,128)(2,1)} %copy-done.69, bf16[1024,128]{1,0:T(8,128)(2,1)} %get-tuple-element.154.aq_ref, ...), custom_call_target="tpu_custom_call" | custom-call | flops 10737418240 | bytes 6815744 | tf_op jit(solution)/shard_map/attend_back/pallas_call | solution.py:37
  316.4 5.4 %collective-permute-done.59 = bf16[2,128,768]{2,1,0:T(8,128)(2,1)S(1)} collective-permute-done((bf16[2,128,768]{2,1,0:T(8,128)(2,1)S(1)}, bf16[2,128,768]{2,1,0:T(8,128)(2,1)S(1)}, u32[]{:S(2)}, u32[]{:S(2)}) %collective-permute-start.59) | collective-permute-done | bytes 393248 | tf_op jit(solution)/shard_map/ppermute | solution.py:60
  367.9 10.2 %collective-permute-done.60 = bf16[4,128,768]{2,1,0:T(8,128)(2,1)S(1)} collective-permute-done((bf16[4,128,768]{2,1,0:T(8,128)(2,1)S(1)}, bf16[4,128,768]{2,1,0:T(8,128)(2,1)S(1)}, u32[]{:S(2)}, u32[]{:S(2)}) %collective-permute-start.60) | collective-permute-done | bytes 786464 | tf_op jit(solution)/shard_map/ppermute | solution.py:60
  388.0 6.8 %collective-permute-done.72 = bf16[128,256]{1,0:T(8,128)(2,1)S(1)} collective-permute-done((bf16[128,256]{1,0:T(8,128)(2,1)S(1)}, bf16[128,256]{1,0:T(8,128)(2,1)S(1)}, u32[]{:S(2)}, u32[]{:S(2)}) %collective-permute-start.72) | collective-permute-done | bytes 65568 | tf_op jit(solution)/shard_map/ppermute | solution.py:60
  399.4 6.1 %collective-permute-done.64 = bf16[128,768]{1,0:T(8,128)(2,1)S(1)} collective-permute-done((bf16[128,768]{1,0:T(8,128)(2,1)S(1)}, bf16[128,768]{1,0:T(8,128)(2,1)S(1)}, u32[]{:S(2)}, u32[]{:S(2)}) %collective-permute-start.64) | collective-permute-done | bytes 196640 | tf_op jit(solution)/shard_map/ppermute | solution.py:60
  429.2 8.8 %collective-permute-done.78 = bf16[4,128,512]{2,1,0:T(8,128)(2,1)S(1)} collective-permute-done((bf16[4,128,512]{2,1,0:T(8,128)(2,1)S(1)}, bf16[4,128,512]{2,1,0:T(8,128)(2,1)S(1)}, u32[]{:S(2)}, u32[]{:S(2)}) %collective-permute-start.78) | collective-permute-done | bytes 524320 | tf_op jit(solution)/shard_map/ppermute | solution.py:60
  455.2 5.0 %collective-permute-done.88 = bf16[256,256]{1,0:T(8,128)(2,1)S(1)} collective-permute-done((bf16[256,256]{1,0:T(8,128)(2,1)S(1)}, bf16[256,256]{1,0:T(8,128)(2,1)S(1)}, u32[]{:S(2)}, u32[]{:S(2)}) %collective-permute-start.88) | collective-permute-done | bytes 131104 | tf_op jit(solution)/shard_map/ppermute | solution.py:60
  (523 shorter events, 256.4 us)
Async XLA Ops:
  0.7 36.3 %collective-permute-start.21 = (bf16[128,256]{1,0:T(8,128)(2,1)}, bf16[128,256]{1,0:T(8,128)(2,1)S(1)}, u32[]{:S(2)}, u32[]{:S(2)}) collective-permute-start(bf16[128,256]{1,0:T(8,128)(2,1)} %param.18), channel_id=1, source_target_pairs={{0,24},{8,16},{16,8},{24,0},{1,25},{9,17},{17,9},{25,1},{2,26},{10... | collective-permute-start | bytes 196616 | tf_op jit(solution)/shard_map/ppermute | solution.py:60
  5.8 31.8 %collective-permute-start.20 = (bf16[128,256]{1,0:T(8,128)(2,1)}, bf16[128,256]{1,0:T(8,128)(2,1)S(1)}, u32[]{:S(2)}, u32[]{:S(2)}) collective-permute-start(bf16[128,256]{1,0:T(8,128)(2,1)} %param.18), channel_id=1, source_target_pairs={{0,16},{8,24},{16,0},{24,8},{1,17},{9,25},{17,1},{25,9},{2,18},{10... | collective-permute-start | bytes 196616 | tf_op jit(solution)/shard_map/ppermute | solution.py:60
  5.8 33.3 %collective-permute-start.19 = (bf16[128,256]{1,0:T(8,128)(2,1)}, bf16[128,256]{1,0:T(8,128)(2,1)S(1)}, u32[]{:S(2)}, u32[]{:S(2)}) collective-permute-start(bf16[128,256]{1,0:T(8,128)(2,1)} %param.18), channel_id=1, source_target_pairs={{0,8},{8,0},{16,24},{24,16},{1,9},{9,1},{17,25},{25,17},{2,10},{10... | collective-permute-start | bytes 196616 | tf_op jit(solution)/shard_map/ppermute | solution.py:60
  8.9 33.8 %collective-permute-start.29 = (bf16[128,512]{1,0:T(8,128)(2,1)}, bf16[128,512]{1,0:T(8,128)(2,1)S(1)}, u32[]{:S(2)}, u32[]{:S(2)}) collective-permute-start(bf16[128,512]{1,0:T(8,128)(2,1)} %param.19), channel_id=1, source_target_pairs={{0,24},{8,16},{16,8},{24,0},{1,25},{9,17},{17,9},{25,1},{2,26},{10... | collective-permute-start | bytes 393224 | tf_op jit(solution)/shard_map/ppermute | solution.py:60
  54.0 30.4 %collective-permute-start = (bf16[256,1024]{1,0:T(8,128)(2,1)S(1)}, bf16[256,1024]{1,0:T(8,128)(2,1)S(1)}, u32[]{:S(2)}, u32[]{:S(2)}) collective-permute-start(bf16[256,1024]{1,0:T(8,128)(2,1)S(1)} %get-tuple-element.117), channel_id=1, source_target_pairs={{0,2},{2,0},{1,3},{3,1},{4,6},{6,4},{5,7},{7,5},{8,10},{10,8},{9,1... | collective-permute-start | bytes 1572872 | tf_op jit(solution)/shard_map/ppermute | solution.py:60
  79.6 34.4 %collective-permute-start.13 = (bf16[4,128,768]{2,1,0:T(8,128)(2,1)S(1)}, bf16[4,128,768]{2,1,0:T(8,128)(2,1)}, u32[]{:S(2)}, u32[]{:S(2)}) collective-permute-start(bf16[4,128,768]{2,1,0:T(8,128)(2,1)S(1)} %pad_maximum_fusion.4.refs_0_), channel_id=1, source_target_pairs={{0,4},{4,0},{1,5},{5,1},{2,6},{6,2},{3,7},{7,3},{8,12},{12,8},{9,1... | collective-permute-start | bytes 2359304 | tf_op jit(solution)/shard_map/ppermute | solution.py:60
  81.7 32.9 %collective-permute-start.14 = (bf16[4,128,768]{2,1,0:T(8,128)(2,1)S(1)}, bf16[4,128,768]{2,1,0:T(8,128)(2,1)}, u32[]{:S(2)}, u32[]{:S(2)}) collective-permute-start(bf16[4,128,768]{2,1,0:T(8,128)(2,1)S(1)} %pad_maximum_fusion.4.refs_0_), channel_id=1, source_target_pairs={{0,2},{2,0},{1,3},{3,1},{4,6},{6,4},{5,7},{7,5},{8,10},{10,8},{9,1... | collective-permute-start | bytes 2359304 | tf_op jit(solution)/shard_map/ppermute | solution.py:60
  85.9 27.5 %collective-permute-start.40 = (bf16[4,256,256]{2,1,0:T(8,128)(2,1)S(1)}, bf16[4,256,256]{2,1,0:T(8,128)(2,1)}, u32[]{:S(2)}, u32[]{:S(2)}) collective-permute-start(bf16[4,256,256]{2,1,0:T(8,128)(2,1)S(1)} %pad_maximum_fusion.8.refs_0_), channel_id=1, source_target_pairs={{0,4},{4,0},{1,5},{5,1},{2,6},{6,2},{3,7},{7,3},{8,12},{12,8},{9,1... | collective-permute-start | bytes 1572872 | tf_op jit(solution)/shard_map/ppermute | solution.py:60
  90.7 72.7 %collective-permute-start.9 = (bf16[512,1024]{1,0:T(8,128)(2,1)S(1)}, bf16[512,1024]{1,0:T(8,128)(2,1)}, u32[]{:S(2)}, u32[]{:S(2)}) collective-permute-start(bf16[512,1024]{1,0:T(8,128)(2,1)S(1)} %pad_maximum_fusion.1.x_ref.refs_9_), channel_id=1, source_target_pairs={{0,1},{1,0},{2,3},{3,2},{4,5},{5,4},{6,7},{7,6},{8,9},{9,8},{10,11... | collective-permute-start | bytes 3145736 | tf_op jit(solution)/shard_map/ppermute | solution.py:60
  123.8 31.4 %collective-permute-start.41 = (bf16[2,256,256]{2,1,0:T(8,128)(2,1)}, bf16[2,256,256]{2,1,0:T(8,128)(2,1)}, u32[]{:S(2)}, u32[]{:S(2)}) collective-permute-start(bf16[2,256,256]{2,1,0:T(8,128)(2,1)} %slice.523), channel_id=1, source_target_pairs={{0,2},{2,0},{1,3},{3,1},{4,6},{6,4},{5,7},{7,5},{8,10},{10,8},{9,1... | collective-permute-start | bytes 786440 | tf_op jit(solution)/shard_map/ppermute | solution.py:60
  125.5 30.8 %collective-permute-start.42 = (bf16[2,256,256]{2,1,0:T(8,128)(2,1)}, bf16[2,256,256]{2,1,0:T(8,128)(2,1)}, u32[]{:S(2)}, u32[]{:S(2)}) collective-permute-start(bf16[2,256,256]{2,1,0:T(8,128)(2,1)} %slice.524), channel_id=1, source_target_pairs={{0,4},{4,0},{1,5},{5,1},{2,6},{6,2},{3,7},{7,3},{8,12},{12,8},{9,1... | collective-permute-start | bytes 786440 | tf_op jit(solution)/shard_map/ppermute | solution.py:60
  126.1 34.9 %collective-permute-start.15 = (bf16[2,128,768]{2,1,0:T(8,128)(2,1)}, bf16[2,128,768]{2,1,0:T(8,128)(2,1)}, u32[]{:S(2)}, u32[]{:S(2)}) collective-permute-start(bf16[2,128,768]{2,1,0:T(8,128)(2,1)} %slice.517), channel_id=1, source_target_pairs={{0,2},{2,0},{1,3},{3,1},{4,6},{6,4},{5,7},{7,5},{8,10},{10,8},{9,1... | collective-permute-start | bytes 1179656 | tf_op jit(solution)/shard_map/ppermute | solution.py:60
  127.5 34.1 %collective-permute-start.16 = (bf16[2,128,768]{2,1,0:T(8,128)(2,1)}, bf16[2,128,768]{2,1,0:T(8,128)(2,1)}, u32[]{:S(2)}, u32[]{:S(2)}) collective-permute-start(bf16[2,128,768]{2,1,0:T(8,128)(2,1)} %slice.518), channel_id=1, source_target_pairs={{0,4},{4,0},{1,5},{5,1},{2,6},{6,2},{3,7},{7,3},{8,12},{12,8},{9,1... | collective-permute-start | bytes 1179656 | tf_op jit(solution)/shard_map/ppermute | solution.py:60
  155.2 37.1 %collective-permute-start.35 = (bf16[256,1024]{1,0:T(8,128)(2,1)S(1)}, bf16[256,1024]{1,0:T(8,128)(2,1)S(1)}, u32[]{:S(2)}, u32[]{:S(2)}) collective-permute-start(bf16[256,1024]{1,0:T(8,128)(2,1)S(1)} %copy-done.86), channel_id=1, source_target_pairs={{0,2},{2,0},{1,3},{3,1},{4,6},{6,4},{5,7},{7,5},{8,10},{10,8},{9,1... | collective-permute-start | bytes 1572872 | tf_op jit(solution)/shard_map/ppermute | solution.py:60
  156.3 42.5 %collective-permute-start.26 = (bf16[2,1024,256]{2,1,0:T(8,128)(2,1)}, bf16[2,1024,256]{2,1,0:T(8,128)(2,1)}, u32[]{:S(2)}, u32[]{:S(2)}) collective-permute-start(bf16[2,1024,256]{2,1,0:T(8,128)(2,1)} %assemble_out.1.refs_4_.refs_2_), channel_id=1, source_target_pairs={{0,1},{1,0},{2,3},{3,2},{4,5},{5,4},{6,7},{7,6},{8,9},{9,8},{10,11... | collective-permute-start | bytes 3145736 | tf_op jit(solution)/shard_map/ppermute | solution.py:60
  161.0 43.0 %collective-permute-start.34 = (bf16[2,1024,512]{2,1,0:T(8,128)(2,1)}, bf16[2,1024,512]{2,1,0:T(8,128)(2,1)}, u32[]{:S(2)}, u32[]{:S(2)}) collective-permute-start(bf16[2,1024,512]{2,1,0:T(8,128)(2,1)} %assemble_up.1.refs_0_), channel_id=1, source_target_pairs={{0,1},{1,0},{2,3},{3,2},{4,5},{5,4},{6,7},{7,6},{8,9},{9,8},{10,11... | collective-permute-start | bytes 6291464 | tf_op jit(solution)/shard_map/ppermute | solution.py:60
  161.5 49.1 %collective-permute-start.43 = (bf16[2,2048,256]{2,1,0:T(8,128)(2,1)S(1)}, bf16[2,2048,256]{2,1,0:T(8,128)(2,1)}, u32[]{:S(2)}, u32[]{:S(2)}) collective-permute-start(bf16[2,2048,256]{2,1,0:T(8,128)(2,1)S(1)} %assemble_down.1.refs_0_), channel_id=1, source_target_pairs={{0,1},{1,0},{2,3},{3,2},{4,5},{5,4},{6,7},{7,6},{8,9},{9,8},{10,11... | collective-permute-start | bytes 6291464 | tf_op jit(solution)/shard_map/ppermute | solution.py:60
  217.7 92.1 %collective-permute-start.44 = (bf16[256,1024]{1,0:T(8,128)(2,1)}, bf16[256,1024]{1,0:T(8,128)(2,1)}, u32[]{:S(2)}, u32[]{:S(2)}) collective-permute-start(bf16[256,1024]{1,0:T(8,128)(2,1)} %get-tuple-element.113), channel_id=1, source_target_pairs={{0,2},{2,0},{1,3},{3,1},{4,6},{6,4},{5,7},{7,5},{8,10},{10,8},{9,1... | collective-permute-start | bytes 1572872 | tf_op jit(solution)/shard_map/ppermute | solution.py:60
  240.5 43.8 %collective-permute-start.45 = (bf16[512,256]{1,0:T(8,128)(2,1)}, bf16[512,256]{1,0:T(8,128)(2,1)S(1)}, u32[]{:S(2)}, u32[]{:S(2)}) collective-permute-start(bf16[512,256]{1,0:T(8,128)(2,1)} %get-tuple-element.66), channel_id=1, source_target_pairs={{0,1},{1,0},{2,3},{3,2},{4,5},{5,4},{6,7},{7,6},{8,9},{9,8},{10,11... | collective-permute-start | bytes 786440 | tf_op jit(solution)/shard_map/ppermute | solution.py:60
  245.0 78.8 %collective-permute-start.66 = (bf16[2,2,4,128,256]{4,3,2,1,0:T(8,128)(2,1)}, bf16[2,2,4,128,256]{4,3,2,1,0:T(8,128)(2,1)}, u32[]{:S(2)}, u32[]{:S(2)}) collective-permute-start(bf16[2,2,4,128,256]{4,3,2,1,0:T(8,128)(2,1)} %get-tuple-element.83), channel_id=1, source_target_pairs={{0,1},{1,0},{2,3},{3,2},{4,5},{5,4},{6,7},{7,6},{8,9},{9,8},{10,11... | collective-permute-start | bytes 3145736 | tf_op jit(solution)/shard_map/ppermute | solution.py:60
  245.4 163.2 %collective-permute-start.74 = (bf16[2,2,4,128,512]{4,3,2,1,0:T(8,128)(2,1)}, bf16[2,2,4,128,512]{4,3,2,1,0:T(8,128)(2,1)}, u32[]{:S(2)}, u32[]{:S(2)}) collective-permute-start(bf16[2,2,4,128,512]{4,3,2,1,0:T(8,128)(2,1)} %get-tuple-element.85), channel_id=1, source_target_pairs={{0,1},{1,0},{2,3},{3,2},{4,5},{5,4},{6,7},{7,6},{8,9},{9,8},{10,11... | collective-permute-start | bytes 6291464 | tf_op jit(solution)/shard_map/ppermute | solution.py:60
  283.1 29.7 %collective-permute-start.61 = (bf16[2,128,768]{2,1,0:T(8,128)(2,1)}, bf16[2,128,768]{2,1,0:T(8,128)(2,1)}, u32[]{:S(2)}, u32[]{:S(2)}) collective-permute-start(bf16[2,128,768]{2,1,0:T(8,128)(2,1)} %get-tuple-element.108), channel_id=1, source_target_pairs={{0,2},{2,0},{1,3},{3,1},{4,6},{6,4},{5,7},{7,5},{8,10},{10,8},{9,1... | collective-permute-start | bytes 1179656 | tf_op jit(solution)/shard_map/ppermute | solution.py:60
  314.9 52.8 %collective-permute-start.62 = (bf16[4,128,768]{2,1,0:T(8,128)(2,1)}, bf16[4,128,768]{2,1,0:T(8,128)(2,1)}, u32[]{:S(2)}, u32[]{:S(2)}) collective-permute-start(bf16[4,128,768]{2,1,0:T(8,128)(2,1)} %pad_maximum_fusion.6), channel_id=1, source_target_pairs={{0,4},{4,0},{1,5},{5,1},{2,6},{6,2},{3,7},{7,3},{8,12},{12,8},{9,1... | collective-permute-start | bytes 2359304 | tf_op jit(solution)/shard_map/ppermute | solution.py:60
  359.1 54.9 %collective-permute-start.82 = (bf16[2,2,4,256,256]{4,3,2,1,0:T(8,128)(2,1)S(1)}, bf16[2,2,4,256,256]{4,3,2,1,0:T(8,128)(2,1)S(1)}, u32[]{:S(2)}, u32[]{:S(2)}) collective-permute-start(bf16[2,2,4,256,256]{4,3,2,1,0:T(8,128)(2,1)S(1)} %copy-done.64), channel_id=1, source_target_pairs={{0,1},{1,0},{2,3},{3,2},{4,5},{5,4},{6,7},{7,6},{8,9},{9,8},{10,11... | collective-permute-start | bytes 6291464 | tf_op jit(solution)/shard_map/ppermute | solution.py:60
  (175 other events, 1732.1 us)
